TPU v7x, 128 devices: a whole 4x4x4 slice. The times are simulated.
128 devices in a mesh: kv: 8 (over y, core), seq: 16 (over x, z).
Axes of the slice: x: 4, y: 4, z: 4, core: 2. Of those that a mesh axis runs over, the one named last changes fastest.
Arguments:
- inputs: bfloat16 [4096, 2048], P('seq'), may hold values from -6 to 6
- cotangent: bfloat16 [4096, 2048], P('seq'), may hold values from -6 to 6
- segment_ids: int32 [4096], replicated, may hold values from 0 to 3, as said below
- attn_gain: bfloat16 [2048], P('seq'), may hold values from 0.5 to 1.5
- query_weight: bfloat16 [2048, 2048], P('seq', 'kv'), may hold values from -0.125 to 0.125
- gate_weight: bfloat16 [2048, 2048], P('seq', 'kv'), may hold values from -0.125 to 0.125
- key_weight: bfloat16 [2048, 1024], P('seq', 'kv'), may hold values from -0.125 to 0.125
- value_weight: bfloat16 [2048, 1024], P('seq', 'kv'), may hold values from -0.125 to 0.125
- output_weight: bfloat16 [2048, 2048], P('kv', 'seq'), may hold values from -0.75 to 0.75
- mlp_gain: bfloat16 [2048], P('seq'), may hold values from 0.5 to 1.5
- mlp_gate: bfloat16 [2048, 6144], P('seq', 'kv'), may hold values from -0.125 to 0.125
- mlp_up: bfloat16 [2048, 6144], P('seq', 'kv'), may hold values from -0.125 to 0.125
- mlp_down: bfloat16 [6144, 2048], P('kv', 'seq'), may hold values from -0.078125 to 0.078125
Outputs:
- block_out: bfloat16 [4096, 2048], P('seq')
- input_grad: float32 [4096, 2048], P('seq')
- attn_gain_grad: float32 [2048], P('seq')
- query_grad: float32 [2048, 2048], P('seq', 'kv')
- gate_grad: float32 [2048, 2048], P('seq', 'kv')
- key_grad: float32 [2048, 1024], P('seq', 'kv')
- value_grad: float32 [2048, 1024], P('seq', 'kv')
- output_grad: float32 [2048, 2048], P('kv', 'seq')
- mlp_gain_grad: float32 [2048], P('seq')
- mlp_gate_grad: float32 [2048, 6144], P('seq', 'kv')
- mlp_up_grad: float32 [2048, 6144], P('seq', 'kv')
- mlp_down_grad: float32 [6144, 2048], P('kv', 'seq')
Inputs may be any that keep to these rules, and one draw needn't show every extreme that they name: `segment_ids`: ids never fall. The packed row holds documents 0, 1 and 2: document 0 ends within the first 256 tokens, document 1 ends within the last 128 tokens, and then document 2 is followed by padding, id 3, of 1 to 64 tokens at the row's end. Every id occurs.
All inputs are finite; a program needn't handle non-finite values.
Results may differ from a plain program's by a relative error of at most 0.024.
Values may be sent and summed in bfloat16 or wider, within the bound.
A program may use at most 128 MiB of HBM per device.

v0:
```python
import jax
import jax.numpy as jnp
from jax import lax
from jax.sharding import PartitionSpec as P

KV_HEADS = 8
HEAD_DIM = 128


epsilon = 1e-06
masked_value = -1e30


def rms_scale(rows_in):
    return lax.rsqrt(jnp.mean(rows_in * rows_in, axis=-1, keepdims=True) + epsilon)


def norm_back(grad_norm, normed, scale_rows, gain):
    scaled = grad_norm * gain
    return scale_rows * (scaled - normed * jnp.mean(scaled * normed, axis=-1, keepdims=True))


def rows_product(left, right):
    return lax.dot_general(
        left, right, (((0,), (0,)), ((), ())), preferred_element_type=jnp.float32
    )


def back_product(left, right):
    return lax.dot_general(
        left, right, (((1,), (1,)), ((), ())), preferred_element_type=jnp.float32
    )


def to_heads(block_in, groups):
    row_count = block_in.shape[0]
    shaped = block_in.reshape(row_count, groups, 2, HEAD_DIM).transpose(1, 2, 0, 3)
    return shaped.reshape(groups, 2 * row_count, HEAD_DIM)


def from_heads(block_in, groups):
    row_count = block_in.shape[1] // 2
    shaped = block_in.reshape(groups, 2, row_count, HEAD_DIM).transpose(2, 0, 1, 3)
    return shaped.reshape(row_count, groups * 2 * HEAD_DIM)


def key_block(keys_values, segment_ids, row_start, row_count, groups):
    block_rows = lax.dynamic_slice_in_dim(keys_values, row_start, row_count, 0)
    width = groups * HEAD_DIM
    key_rows = block_rows[:, :width].reshape(row_count, groups, HEAD_DIM)
    value_rows = block_rows[:, width:].reshape(row_count, groups, HEAD_DIM)
    key_segment = lax.dynamic_slice_in_dim(segment_ids, row_start, row_count, 0)
    key_place = row_start + lax.iota(jnp.int32, row_count)
    return (key_rows, value_rows, key_segment, key_place)


def block_scores(queries, query_segment, query_place, block):
    key_rows, value_rows, key_segment, key_place = block
    scores = jnp.einsum(
        "gqd,kgd->gqk", queries, key_rows, preferred_element_type=jnp.float32
    ) * HEAD_DIM ** (-0.5)
    allowed = (query_segment[:, None] == key_segment[None, :]) & (
        query_place[:, None] >= key_place[None, :]
    )
    return (scores, allowed)


def block_probs(queries, query_segment, query_place, block, log_total):
    scores, allowed = block_scores(queries, query_segment, query_place, block)
    return jnp.exp(jnp.where(allowed, scores - log_total[..., None], masked_value))


def per_device(
    inputs,
    cotangent,
    segment_ids,
    attn_gain,
    query_weight,
    gate_weight,
    key_weight,
    value_weight,
    output_weight,
    mlp_gain,
    mlp_gate,
    mlp_up,
    mlp_down,
):
    groups = KV_HEADS // lax.axis_size("kv")
    local_rows = inputs.shape[0]
    total_rows = segment_ids.shape[0]
    key_span = min(512, total_rows)
    row_first = lax.axis_index("seq") * local_rows
    local_segment = lax.dynamic_slice_in_dim(segment_ids, row_first, local_rows, 0)
    local_place = row_first + lax.iota(jnp.int32, local_rows)
    query_segment = jnp.concatenate([local_segment, local_segment])
    query_place = jnp.concatenate([local_place, local_place])
    segment_first = jnp.sum((segment_ids < local_segment[0]).astype(jnp.int32))
    block_first = segment_first // key_span
    block_after = (row_first + local_rows - 1) // key_span + 1
    w_query, w_gate, w_key, w_value, gain_one, w_out = (
        lax.all_gather(query_weight, "seq", axis=0, tiled=True),
        lax.all_gather(gate_weight, "seq", axis=0, tiled=True),
        lax.all_gather(key_weight, "seq", axis=0, tiled=True),
        lax.all_gather(value_weight, "seq", axis=0, tiled=True),
        lax.all_gather(attn_gain, "seq", axis=0, tiled=True),
        lax.all_gather(output_weight, "seq", axis=1, tiled=True),
    )
    x_float = inputs.astype(jnp.float32)
    scale_one = rms_scale(x_float)
    plain_one = x_float * scale_one
    x_norm = (plain_one * gain_one.astype(jnp.float32)).astype(jnp.bfloat16)
    query_local = jnp.dot(x_norm, w_query, preferred_element_type=jnp.float32).astype(jnp.bfloat16)
    key_local = jnp.dot(x_norm, w_key, preferred_element_type=jnp.float32).astype(jnp.bfloat16)
    value_local = jnp.dot(x_norm, w_value, preferred_element_type=jnp.float32).astype(jnp.bfloat16)
    gate_pre = jnp.dot(x_norm, w_gate, preferred_element_type=jnp.float32)
    keys_values = lax.all_gather(
        jnp.concatenate([key_local, value_local], axis=1), "seq", axis=0, tiled=True
    )
    queries = to_heads(query_local, groups)

    def max_step(block_index, state_pair):
        running_max, running_sum = state_pair
        block = key_block(keys_values, segment_ids, block_index * key_span, key_span, groups)
        scores, allowed = block_scores(queries, query_segment, query_place, block)
        masked = jnp.where(allowed, scores, masked_value)
        new_max = jnp.maximum(running_max, jnp.max(masked, axis=-1))
        shifted = jnp.where(allowed, jnp.exp(masked - new_max[..., None]), 0.0)
        new_sum = running_sum * jnp.exp(running_max - new_max) + jnp.sum(shifted, axis=-1)
        return (new_max, new_sum)

    start_max = jnp.full((groups, 2 * local_rows), masked_value, jnp.float32)
    final_state = lax.fori_loop(
        block_first, block_after, max_step, (start_max, jnp.zeros_like(start_max))
    )
    log_total = final_state[0] + jnp.log(final_state[1])

    def out_step(block_index, summed):
        block = key_block(keys_values, segment_ids, block_index * key_span, key_span, groups)
        probs = block_probs(queries, query_segment, query_place, block, log_total)
        return summed + jnp.einsum(
            "gqk,kgd->gqd", probs.astype(jnp.bfloat16), block[1], preferred_element_type=jnp.float32
        )

    attn_heads = lax.fori_loop(
        block_first, block_after, out_step, jnp.zeros(queries.shape, jnp.float32)
    )
    attn_rows = from_heads(attn_heads, groups)
    gate_sig = jax.nn.sigmoid(gate_pre)
    gated = (attn_rows * gate_sig).astype(jnp.bfloat16)
    attn_out = lax.psum(
        jnp.dot(gated, w_out, preferred_element_type=jnp.float32).astype(jnp.bfloat16), "kv"
    ).astype(jnp.float32)
    mid_rows = x_float + attn_out
    w_mlp_gate, w_mlp_up, gain_two, w_down = (
        lax.all_gather(mlp_gate, "seq", axis=0, tiled=True),
        lax.all_gather(mlp_up, "seq", axis=0, tiled=True),
        lax.all_gather(mlp_gain, "seq", axis=0, tiled=True),
        lax.all_gather(mlp_down, "seq", axis=1, tiled=True),
    )
    scale_two = rms_scale(mid_rows)
    plain_two = mid_rows * scale_two
    h_norm = (plain_two * gain_two.astype(jnp.float32)).astype(jnp.bfloat16)
    gate_mlp = jnp.dot(h_norm, w_mlp_gate, preferred_element_type=jnp.float32)
    up_mlp = jnp.dot(h_norm, w_mlp_up, preferred_element_type=jnp.float32)
    gate_sigmoid = jax.nn.sigmoid(gate_mlp)
    silu_gate = gate_mlp * gate_sigmoid
    mixed = (silu_gate * up_mlp).astype(jnp.bfloat16)
    mlp_out = lax.psum(
        jnp.dot(mixed, w_down, preferred_element_type=jnp.float32).astype(jnp.bfloat16), "kv"
    ).astype(jnp.float32)
    block_out = (mid_rows + mlp_out).astype(jnp.bfloat16)
    w_mlp_gate, w_mlp_up, gain_two, w_down = (
        lax.all_gather(mlp_gate, "seq", axis=0, tiled=True),
        lax.all_gather(mlp_up, "seq", axis=0, tiled=True),
        lax.all_gather(mlp_gain, "seq", axis=0, tiled=True),
        lax.all_gather(mlp_down, "seq", axis=1, tiled=True),
    )
    keep_rows = (local_segment != jnp.max(segment_ids)).astype(jnp.float32)
    grad_out = (cotangent.astype(jnp.float32) * keep_rows[:, None]).astype(jnp.bfloat16)
    grad_mixed = back_product(grad_out, w_down)
    grad_gate = (
        grad_mixed * up_mlp * gate_sigmoid * (1.0 + gate_mlp * (1.0 - gate_sigmoid))
    ).astype(jnp.bfloat16)
    grad_up = (grad_mixed * silu_gate).astype(jnp.bfloat16)
    grad_hnorm = lax.psum(
        back_product(grad_gate, w_mlp_gate) + back_product(grad_up, w_mlp_up), "kv"
    )
    mlp_terms = (
        lax.psum_scatter(
            rows_product(h_norm, grad_gate).astype(jnp.bfloat16),
            "seq",
            scatter_dimension=0,
            tiled=True,
        ).astype(jnp.float32),
        lax.psum_scatter(
            rows_product(h_norm, grad_up).astype(jnp.bfloat16),
            "seq",
            scatter_dimension=0,
            tiled=True,
        ).astype(jnp.float32),
        lax.psum_scatter(
            rows_product(mixed, grad_out).astype(jnp.bfloat16),
            "seq",
            scatter_dimension=1,
            tiled=True,
        ).astype(jnp.float32),
    )
    mlp_gate_grad, mlp_up_grad, mlp_down_grad = mlp_terms
    gain_two_term = jnp.sum(grad_hnorm * plain_two, axis=0)
    grad_mid = grad_out.astype(jnp.float32) + norm_back(
        grad_hnorm, plain_two, scale_two, gain_two.astype(jnp.float32)
    )
    grad_attn = grad_mid.astype(jnp.bfloat16)
    w_query, w_gate, w_key, w_value, gain_one, w_out = (
        lax.all_gather(query_weight, "seq", axis=0, tiled=True),
        lax.all_gather(gate_weight, "seq", axis=0, tiled=True),
        lax.all_gather(key_weight, "seq", axis=0, tiled=True),
        lax.all_gather(value_weight, "seq", axis=0, tiled=True),
        lax.all_gather(attn_gain, "seq", axis=0, tiled=True),
        lax.all_gather(output_weight, "seq", axis=1, tiled=True),
    )
    grad_gated = back_product(grad_attn, w_out)
    out_term = rows_product(gated, grad_attn)
    grad_heads_out = (grad_gated * gate_sig).astype(jnp.bfloat16)
    grad_gate_attn = (grad_gated * attn_rows * gate_sig * (1.0 - gate_sig)).astype(jnp.bfloat16)
    grad_outer = to_heads(grad_heads_out, groups)

    def dot_step(block_index, summed):
        block = key_block(keys_values, segment_ids, block_index * key_span, key_span, groups)
        probs = block_probs(queries, query_segment, query_place, block, log_total)
        grad_probs = jnp.einsum(
            "gqd,kgd->gqk", grad_outer, block[1], preferred_element_type=jnp.float32
        )
        return summed + jnp.sum(probs * grad_probs, axis=-1)

    row_dots = lax.fori_loop(
        block_first, block_after, dot_step, jnp.zeros(log_total.shape, jnp.float32)
    )
    kv_width = groups * HEAD_DIM

    def grad_step(block_index, carried):
        grad_q_heads, kv_buffer = carried
        row_start = block_index * key_span
        block = key_block(keys_values, segment_ids, row_start, key_span, groups)
        probs = block_probs(queries, query_segment, query_place, block, log_total)
        grad_probs = jnp.einsum(
            "gqd,kgd->gqk", grad_outer, block[1], preferred_element_type=jnp.float32
        )
        grad_scores = (probs * (grad_probs - row_dots[..., None]) * HEAD_DIM ** (-0.5)).astype(
            jnp.bfloat16
        )
        grad_q_heads = grad_q_heads + jnp.einsum(
            "gqk,kgd->gqd", grad_scores, block[0], preferred_element_type=jnp.float32
        )
        grad_keys = jnp.einsum(
            "gqk,gqd->kgd", grad_scores, queries, preferred_element_type=jnp.float32
        )
        grad_values = jnp.einsum(
            "gqk,gqd->kgd",
            probs.astype(jnp.bfloat16),
            grad_outer,
            preferred_element_type=jnp.float32,
        )
        rows_new = jnp.concatenate(
            [grad_keys.reshape(key_span, kv_width), grad_values.reshape(key_span, kv_width)], axis=1
        )
        kv_buffer = lax.dynamic_update_slice_in_dim(kv_buffer, rows_new, row_start, 0)
        return (grad_q_heads, kv_buffer)

    start_grads = (
        jnp.zeros(queries.shape, jnp.float32),
        jnp.zeros((total_rows, 2 * kv_width), jnp.float32),
    )
    grad_q_heads, kv_buffer = lax.fori_loop(block_first, block_after, grad_step, start_grads)
    grad_query = from_heads(grad_q_heads, groups).astype(jnp.bfloat16)
    grad_kv = lax.psum_scatter(
        kv_buffer.astype(jnp.bfloat16), "seq", scatter_dimension=0, tiled=True
    ).astype(jnp.float32)
    grad_key = grad_kv[:, :kv_width].astype(jnp.bfloat16)
    grad_value = grad_kv[:, kv_width:].astype(jnp.bfloat16)
    grad_xpart = back_product(grad_query, w_query) + back_product(grad_key, w_key)
    grad_xpart = (
        grad_xpart + back_product(grad_value, w_value) + back_product(grad_gate_attn, w_gate)
    )
    grad_xnorm = lax.psum(grad_xpart.astype(jnp.bfloat16), "kv").astype(jnp.float32)
    attn_terms = (
        lax.psum_scatter(
            rows_product(x_norm, grad_query).astype(jnp.bfloat16),
            "seq",
            scatter_dimension=0,
            tiled=True,
        ).astype(jnp.float32),
        lax.psum_scatter(
            rows_product(x_norm, grad_gate_attn).astype(jnp.bfloat16),
            "seq",
            scatter_dimension=0,
            tiled=True,
        ).astype(jnp.float32),
        lax.psum_scatter(
            rows_product(x_norm, grad_key).astype(jnp.bfloat16),
            "seq",
            scatter_dimension=0,
            tiled=True,
        ).astype(jnp.float32),
        lax.psum_scatter(
            rows_product(x_norm, grad_value).astype(jnp.bfloat16),
            "seq",
            scatter_dimension=0,
            tiled=True,
        ).astype(jnp.float32),
        lax.psum_scatter(
            out_term.astype(jnp.bfloat16), "seq", scatter_dimension=1, tiled=True
        ).astype(jnp.float32),
        lax.psum_scatter(
            jnp.sum(grad_xnorm * plain_one, axis=0).astype(jnp.bfloat16),
            "seq",
            scatter_dimension=0,
            tiled=True,
        ).astype(jnp.float32),
        lax.psum_scatter(
            gain_two_term.astype(jnp.bfloat16), "seq", scatter_dimension=0, tiled=True
        ).astype(jnp.float32),
    )
    input_grad = grad_mid + norm_back(
        grad_xnorm, plain_one, scale_one, gain_one.astype(jnp.float32)
    )
    return (
        block_out,
        input_grad,
        attn_terms[5],
        attn_terms[0],
        attn_terms[1],
        attn_terms[2],
        attn_terms[3],
        attn_terms[4],
        attn_terms[6],
        mlp_gate_grad,
        mlp_up_grad,
        mlp_down_grad,
    )


def solution(mesh):
    return jax.shard_map(
        per_device,
        mesh=mesh,
        in_specs=(
            P("seq", None),
            P("seq", None),
            P(),
            P("seq"),
            P("seq", "kv"),
            P("seq", "kv"),
            P("seq", "kv"),
            P("seq", "kv"),
            P("kv", "seq"),
            P("seq"),
            P("seq", "kv"),
            P("seq", "kv"),
            P("kv", "seq"),
        ),
        out_specs=(
            P("seq", None),
            P("seq", None),
            P("seq"),
            P("seq", "kv"),
            P("seq", "kv"),
            P("seq", "kv"),
            P("seq", "kv"),
            P("kv", "seq"),
            P("seq"),
            P("seq", "kv"),
            P("seq", "kv"),
            P("kv", "seq"),
        ),
        check_vma=False,
    )
```

profile of v0, /device:TPU:1, one launch (start us, length us, event | category | flops | bytes accessed | tf_op | source)
XLA Modules:
  0.0 1352.1 jit_solution(5517419662253377424)
XLA Ops:
  8.0 18.3 %all-gather = bf16[16,1,128]{2,1,0:T(2,128)(2,1)S(1)} all-gather(bf16[1,1,128]{2,1,0:T(2,128)(2,1)} %bitcast.238), channel_id=1, replica_groups=mesh['kv'=8,'seq'=16] {'seq'}, dimensions={0}, use_global_device_ids=true | all-gather | bytes 4352 | tf_op jit(solution)/shard_map/all_gather | solution.py:105
  26.3 17.9 %all_gather.44 = bf16[2048,128]{1,0:T(8,128)(2,1)S(1)} all-gather(bf16[128,128]{1,0:T(8,128)(2,1)} %param.27), channel_id=1, replica_groups=mesh['kv'=8,'seq'=16] {'seq'}, dimensions={0}, use_global_device_ids=true | all-gather | bytes 557056 | tf_op jit(solution)/shard_map/all_gather | solution.py:103
  44.2 17.4 %all_gather.45 = bf16[2048,128]{1,0:T(8,128)(2,1)S(1)} all-gather(bf16[128,128]{1,0:T(8,128)(2,1)} %param.28), channel_id=1, replica_groups=mesh['kv'=8,'seq'=16] {'seq'}, dimensions={0}, use_global_device_ids=true | all-gather | bytes 557056 | tf_op jit(solution)/shard_map/all_gather | solution.py:104
  71.1 1.9 convolution_convert_fusion.10
  73.1 53.3 %all-gather.10.cloned.1.call-done = bf16[4096,256]{0,1:T(8,128)(2,1)} async-done(((bf16[256,256]{0,1:T(8,128)(2,1)}), bf16[4096,256]{0,1:T(8,128)(2,1)}) %all-gather.10.cloned.1.call-update) | async-done | bytes 2097168 | tf_op jit(solution)/shard_map/all_gather | solution.py:116
  126.5 3.3 copy.53
  131.4 2.5 while.45
  131.5 2.4 fusion.171
  133.9 2.0 copy.54
  135.9 34.3 %all-gather.14.cloned.1.call-done = bf16[2048,256]{1,0:T(8,128)(2,1)} async-done(((bf16[128,256]{1,0:T(8,128)(2,1)}), bf16[2048,256]{1,0:T(8,128)(2,1)}) %all-gather.14.cloned.1.call-update) | async-done | bytes 1048592 | tf_op jit(solution)/shard_map/all_gather | solution.py:102
  170.2 2.6 fusion.84
  172.8 42.2 %all-gather.16.cloned.1.call-done = bf16[256,2048]{1,0:T(8,128)(2,1)} async-done(((bf16[256,128]{1,0:T(8,128)(2,1)}), bf16[256,2048]{1,0:T(8,128)(2,1)}) %all-gather.16.cloned.1.call-update) | async-done | bytes 1048592 | tf_op jit(solution)/shard_map/all_gather | solution.py:106
  215.0 2.7 convolution_convert_fusion.6
  219.8 15.6 %all-gather.1 = bf16[16,1,128]{2,1,0:T(2,128)(2,1)S(1)} all-gather(bf16[1,1,128]{2,1,0:T(2,128)(2,1)S(1)} %bitcast.239), channel_id=1, replica_groups=mesh['kv'=8,'seq'=16] {'seq'}, dimensions={0}, use_global_device_ids=true | all-gather | bytes 4352 | tf_op jit(solution)/shard_map/all_gather | solution.py:157
  236.2 42.7 %all-reduce.8.cloned.1.call-done = bf16[256,2048]{1,0:T(8,128)(2,1)} async-done(((bf16[256,2048]{1,0:T(8,128)(2,1)}), bf16[256,2048]{1,0:T(8,128)(2,1)}) %all-reduce.8.cloned.1.call-update) | async-done | bytes 1048592 | tf_op jit(solution)/shard_map/psum | solution.py:150
  278.9 1.7 multiply_reduce_fusion.2
  281.2 48.9 %all-gather.20.cloned.1.call-done = bf16[2048,768]{1,0:T(8,128)(2,1)} async-done(((bf16[128,768]{1,0:T(8,128)(2,1)}), bf16[2048,768]{1,0:T(8,128)(2,1)}) %all-gather.20.cloned.1.call-update) | async-done | bytes 3145744 | tf_op jit(solution)/shard_map/all_gather | solution.py:156
  330.1 3.7 fusion.104
  333.8 45.4 %all-gather.18.cloned.1.call-done = bf16[2048,768]{1,0:T(8,128)(2,1)} async-done(((bf16[128,768]{1,0:T(8,128)(2,1)}), bf16[2048,768]{1,0:T(8,128)(2,1)}) %all-gather.18.cloned.1.call-update) | async-done | bytes 3145744 | tf_op jit(solution)/shard_map/all_gather | solution.py:155
  379.2 3.7 fusion.103
  382.9 49.4 %all-gather.22.cloned.1.call-done = bf16[768,2048]{1,0:T(8,128)(2,1)} async-done(((bf16[768,128]{1,0:T(8,128)(2,1)}), bf16[768,2048]{1,0:T(8,128)(2,1)}) %all-gather.22.cloned.1.call-update) | async-done | bytes 3145744 | tf_op jit(solution)/shard_map/all_gather | solution.py:158
  432.3 4.8 multiply_convert_fusion.2
  439.3 2.4 convolution_add_fusion
  441.7 63.9 %all-reduce.10.cloned.1.call-done = f32[256,2048]{1,0:T(8,128)} async-done(((f32[256,2048]{1,0:T(8,128)}), f32[256,2048]{1,0:T(8,128)}) %all-reduce.10.cloned.1.call-update) | async-done | bytes 2097168 | tf_op jit(solution)/shard_map/psum | solution.py:185
  505.6 2.5 multiply_reduce_fusion
  511.1 3.4 while.46
  516.7 6.1 while.47
  525.1 2.3 copy.59
  533.4 129.8 %reduce-scatter.14.cloned.1.call-done = bf16[256,256]{0,1:T(8,128)(2,1)} async-done(((bf16[4096,256]{0,1:T(8,128)(2,1)}), bf16[256,256]{0,1:T(8,128)(2,1)}) %reduce-scatter.14.cloned.1.call-update) | async-done | bytes 131088 | tf_op jit(solution)/shard_map/reduce_scatter | solution.py:276
  663.3 2.2 convolution_convert_fusion.9
  665.6 3.9 convolution_convert_fusion.7
  671.0 1.8 fusion.106
  677.2 4.0 convolution_convert_fusion
  681.2 4.7 copy.61
  686.9 4.0 convolution_convert_fusion.1
  691.9 4.0 convolution_convert_fusion.2
  697.7 41.4 %reduce-scatter.28.cloned.1.call-done = bf16[128,256]{1,0:T(8,128)(2,1)} async-done(((bf16[2048,256]{1,0:T(8,128)(2,1)}), bf16[128,256]{1,0:T(8,128)(2,1)}) %reduce-scatter.28.cloned.1.call-update) | async-done | bytes 65552
  740.8 73.8 %reduce-scatter.18.cloned.1.call-done = bf16[128,256]{1,0:T(8,128)(2,1)} async-done(((bf16[2048,256]{1,0:T(8,128)(2,1)}), bf16[128,256]{1,0:T(8,128)(2,1)}) %reduce-scatter.18.cloned.1.call-update) | async-done | bytes 65552 | tf_op jit(solution)/shard_map/reduce_scatter | solution.py:293
  816.0 74.4 %reduce-scatter.16.cloned.1.call-done = bf16[128,256]{1,0:T(8,128)(2,1)} async-done(((bf16[2048,256]{1,0:T(8,128)(2,1)}), bf16[128,256]{1,0:T(8,128)(2,1)}) %reduce-scatter.16.cloned.1.call-update) | async-done | bytes 65552 | tf_op jit(solution)/shard_map/reduce_scatter | solution.py:287
  891.9 73.2 %reduce-scatter.20.cloned.1.call-done = bf16[128,128]{1,0:T(8,128)(2,1)} async-done(((bf16[2048,128]{1,0:T(8,128)(2,1)}), bf16[128,128]{1,0:T(8,128)(2,1)}) %reduce-scatter.20.cloned.1.call-update) | async-done | bytes 32784 | tf_op jit(solution)/shard_map/reduce_scatter | solution.py:299
  966.6 73.8 %reduce-scatter.22.cloned.1.call-done = bf16[128,128]{1,0:T(8,128)(2,1)} async-done(((bf16[2048,128]{1,0:T(8,128)(2,1)}), bf16[128,128]{1,0:T(8,128)(2,1)}) %reduce-scatter.22.cloned.1.call-update) | async-done | bytes 32784 | tf_op jit(solution)/shard_map/reduce_scatter | solution.py:305
  1041.7 66.2 %all-reduce.12.cloned.1.call-done = (bf16[256,2048]{1,0:T(8,128)(2,1)}, bf16[256,2048]{1,0:T(8,128)(2,1)}) async-done(((bf16[256,2048]{1,0:T(8,128)(2,1)}, bf16[256,2048]{1,0:T(8,128)(2,1)}), (bf16[256,2048]{1,0:T(8,128)(2,1)}, bf16[256,2048]{1,0:T(8,128)(2,1)})) %all-reduce.12.cloned.1.call-update) | async-done | bytes 2097168 | tf_op jit(solution)/shard_map/psum | solution.py:168
  1108.0 2.0 fusion.74
  1110.0 34.0 %all-reduce.2 = (bf16[2048]{0:T(1024)(128)(2,1)S(1)}, bf16[2048]{0:T(1024)(128)(2,1)S(1)}) all-reduce(bf16[2048]{0:T(1024)(128)(2,1)S(1)} %get-tuple-element.394, bf16[2048]{0:T(1024)(128)(2,1)S(1)} %get-tuple-element.392), channel_id=3, replica_groups=mesh['kv'=8,'seq'=16] {'seq'}, use_global_device_ids=true, to_apply=%region_23.24.clone | all-reduce | flops 4096 | bytes 16384
  1145.2 4.7 fusion.71
  1149.9 37.1 %reduce-scatter.30.cloned.1.call-done = bf16[128,768]{1,0:T(8,128)(2,1)} async-done(((bf16[2048,768]{1,0:T(8,128)(2,1)}), bf16[128,768]{1,0:T(8,128)(2,1)}) %reduce-scatter.30.cloned.1.call-update) | async-done | bytes 196624
  1188.9 76.5 %reduce-scatter.26.cloned.1.call-done = bf16[128,768]{1,0:T(8,128)(2,1)} async-done(((bf16[2048,768]{1,0:T(8,128)(2,1)}), bf16[128,768]{1,0:T(8,128)(2,1)}) %reduce-scatter.26.cloned.1.call-update) | async-done | bytes 196624 | tf_op jit(solution)/shard_map/reduce_scatter | solution.py:195
  1267.1 76.8 %reduce-scatter.24.cloned.1.call-done = bf16[128,768]{1,0:T(8,128)(2,1)} async-done(((bf16[2048,768]{1,0:T(8,128)(2,1)}), bf16[128,768]{1,0:T(8,128)(2,1)}) %reduce-scatter.24.cloned.1.call-update) | async-done | bytes 196624 | tf_op jit(solution)/shard_map/reduce_scatter | solution.py:189
  (199 shorter events, 61.3 us)
Async XLA Ops:
  7.2 56.1 %copy-start = (bf16[256,2048]{1,0:T(8,128)(2,1)S(1)}, bf16[256,2048]{1,0:T(8,128)(2,1)}, u32[]{:S(2)}) copy-start(bf16[256,2048]{1,0:T(8,128)(2,1)} %param.21) | copy-start | bytes 3145732
  7.2 63.9 %all-gather.12.cloned.1.call-start = ((), (), s32[]{:S(2)}) async-start(), calls=%async_computation.10 | async-start | bytes 1114112 | tf_op jit(solution)/shard_map/all_gather | solution.py:101
  7.9 118.5 %all-gather.10.cloned.1.call-start = ((), (), s32[]{:S(2)}) async-start(), calls=%async_computation.9 | async-start | bytes 2228224 | tf_op jit(solution)/shard_map/all_gather | solution.py:116
  26.2 143.9 %copy-start.33 = (f32[16,1,128]{2,1,0:T(1,128)}, f32[16,1,128]{2,1,0:T(1,128)S(1)}, u32[]{:S(2)}) copy-start(f32[16,1,128]{2,1,0:T(1,128)S(1)} %convert_element_type.225) | copy-start | bytes 24580
  44.2 20.3 %copy-start.14 = (bf16[2048,128]{1,0:T(8,128)(2,1)}, bf16[2048,128]{1,0:T(8,128)(2,1)S(1)}, u32[]{:S(2)}) copy-start(bf16[2048,128]{1,0:T(8,128)(2,1)S(1)} %all_gather.44) | copy-start | bytes 1572868
  61.6 2.9 copy-start.12
  63.3 106.9 %copy-start.35 = (f32[256]{0:T(256)}, f32[256]{0:T(256)S(1)}, u32[]{:S(2)}) copy-start(f32[256]{0:T(256)S(1)} %add_rsqrt_fusion.1) | copy-start | bytes 3076
  63.3 3.2 copy-start.29
  65.2 105.0 %all-gather.14.cloned.1.call-start = ((), (), s32[]{:S(2)}) async-start(), calls=%async_computation.11 | async-start | bytes 1114112 | tf_op jit(solution)/shard_map/all_gather | solution.py:102
  65.9 149.1 %all-gather.16.cloned.1.call-start = ((), (), s32[]{:S(2)}) async-start(), calls=%async_computation.12 | async-start | bytes 1114112 | tf_op jit(solution)/shard_map/all_gather | solution.py:106
  66.5 212.4 %all-reduce.8.cloned.1.call-start = ((), (), s32[]{:S(2)}) async-start(), calls=%async_computation.13 | async-start | bytes 2097152 | tf_op jit(solution)/shard_map/psum | solution.py:150
  133.9 2.0 copy-start.40
  133.9 38.9 %copy-start.5 = (bf16[4096,256]{1,0:T(8,128)(2,1)}, bf16[4096,256]{1,0:T(8,128)(2,1)S(1)}, u32[]{:S(2)}) copy-start(bf16[4096,256]{1,0:T(8,128)(2,1)S(1)} %get-tuple-element.960) | copy-start | bytes 6291460
  133.9 101.5 %copy-start.30 = (s32[4096]{0:T(1024)}, s32[4096]{0:T(1024)S(1)}, u32[]{:S(2)}) copy-start(s32[4096]{0:T(1024)S(1)} %get-tuple-element.992) | copy-start | bytes 49156
  172.8 107.8 %copy-start.23 = (bf16[256,256]{0,1:T(8,128)(2,1)}, bf16[256,256]{0,1:T(8,128)(2,1)S(1)}, u32[]{:S(2)}) copy-start(bf16[256,256]{0,1:T(8,128)(2,1)S(1)} %get-tuple-element.491) | copy-start | bytes 393220
  172.8 47.0 %copy-start.41 = (bf16[128]{0:T(256)(128)(2,1)S(1)}, bf16[128]{0:T(256)(128)(2,1)}, u32[]{:S(2)}) copy-start(bf16[128]{0:T(256)(128)(2,1)} %param.30) | copy-start | bytes 772
  217.7 112.4 %all-gather.20.cloned.1.call-start = ((), (), s32[]{:S(2)}) async-start(), calls=%async_computation.15 | async-start | bytes 3342336 | tf_op jit(solution)/shard_map/all_gather | solution.py:156
  218.2 160.9 %all-gather.18.cloned.1.call-start = ((), (), s32[]{:S(2)}) async-start(), calls=%async_computation.14 | async-start | bytes 3342336 | tf_op jit(solution)/shard_map/all_gather | solution.py:155
  219.0 213.3 %all-gather.22.cloned.1.call-start = ((), (), s32[]{:S(2)}) async-start(), calls=%async_computation.16 | async-start | bytes 3342336 | tf_op jit(solution)/shard_map/all_gather | solution.py:158
  219.7 285.9 %all-reduce.10.cloned.1.call-start = ((), (), s32[]{:S(2)}) async-start(), calls=%async_computation.17 | async-start | bytes 4194304 | tf_op jit(solution)/shard_map/psum | solution.py:185
  236.2 272.0 %copy-start.38 = (f32[256]{0:T(256)}, f32[256]{0:T(256)S(1)}, u32[]{:S(2)}) copy-start(f32[256]{0:T(256)S(1)} %compare_convert_fusion) | copy-start | bytes 3076
  278.9 1.8 copy-start.1
  281.1 98.0 %copy-start.3 = (bf16[256,2048]{1,0:T(8,128)(2,1)}, bf16[256,2048]{1,0:T(8,128)(2,1)S(1)}, u32[]{:S(2)}) copy-start(bf16[256,2048]{1,0:T(8,128)(2,1)S(1)} %multiply_convert_fusion.1) | copy-start | bytes 3145732
  432.3 4.8 copy-start.11
  437.1 2.2 copy-start.10
  441.7 221.6 %reduce-scatter.14.cloned.1.call-start = ((), (), s32[]{:S(2)}) async-start(), calls=%async_computation.18 | async-start | bytes 2228224 | tf_op jit(solution)/shard_map/reduce_scatter | solution.py:276
  505.6 2.5 copy-start.2
  505.6 2.6 copy-start.4
  505.6 2.8 copy-start.8
  508.4 1.3 copy-start.28
  518.9 1.5 copy-start.7
  522.8 216.3 %reduce-scatter.28.cloned.1.call-start = ((), (), s32[]{:S(2)}) async-start(), calls=%async_computation.25 | async-start | bytes 1114112
  525.1 2.4 copy-start.25
  525.1 2.4 copy-start.34
  525.1 2.4 copy-start.36
  527.5 287.1 %reduce-scatter.18.cloned.1.call-start = ((), (), s32[]{:S(2)}) async-start(), calls=%async_computation.20 | async-start | bytes 1114112 | tf_op jit(solution)/shard_map/reduce_scatter | solution.py:293
  529.2 361.3 %reduce-scatter.16.cloned.1.call-start = ((), (), s32[]{:S(2)}) async-start(), calls=%async_computation.19 | async-start | bytes 1114112 | tf_op jit(solution)/shard_map/reduce_scatter | solution.py:287
  533.1 132.4 %copy-start.20 = (bf16[256,768]{1,0:T(8,128)(2,1)S(1)}, bf16[256,768]{1,0:T(8,128)(2,1)}, u32[]{:S(2)}) copy-start(bf16[256,768]{1,0:T(8,128)(2,1)} %get-tuple-element.486) | copy-start | bytes 1179652
  533.2 432.0 %reduce-scatter.20.cloned.1.call-start = ((), (), s32[]{:S(2)}) async-start(), calls=%async_computation.21 | async-start | bytes 557056 | tf_op jit(solution)/shard_map/reduce_scatter | solution.py:299
  665.5 374.8 %reduce-scatter.22.cloned.1.call-start = ((), (), s32[]{:S(2)}) async-start(), calls=%async_computation.22 | async-start | bytes 557056 | tf_op jit(solution)/shard_map/reduce_scatter | solution.py:305
  665.6 3.9 copy-start.31
  670.9 437.1 %all-reduce.12.cloned.1.call-start = ((), (), s32[]{:S(2)}) async-start(), calls=%async_computation.27 | async-start | bytes 4194304 | tf_op jit(solution)/shard_map/psum | solution.py:168
  671.0 1.9 copy-start.15
  671.0 1.9 copy-start.32
  676.6 510.4 %reduce-scatter.30.cloned.1.call-start = ((), (), s32[]{:S(2)}) async-start(), calls=%async_computation.26 | async-start | bytes 3342336
  686.0 579.4 %reduce-scatter.26.cloned.1.call-start = ((), (), s32[]{:S(2)}) async-start(), calls=%async_computation.24 | async-start | bytes 3342336 | tf_op jit(solution)/shard_map/reduce_scatter | solution.py:195
  690.9 652.9 %reduce-scatter.24.cloned.1.call-start = ((), (), s32[]{:S(2)}) async-start(), calls=%async_computation.23 | async-start | bytes 3342336 | tf_op jit(solution)/shard_map/reduce_scatter | solution.py:189
  695.8 412.1 %copy-start.37 = (f32[256]{0:T(256)S(1)}, f32[256]{0:T(256)}, u32[]{:S(2)}) copy-start(f32[256]{0:T(256)} %copy-done.35) | copy-start | bytes 3076
  (14 other events, 13.6 us)
Sparse Core Ops, SparseCore 0:
  10.2 44.7 all-gather.11
  65.3 61.1 all-gather.9
  128.6 41.5 all-gather.13
  172.1 42.8 all-gather.15
  217.8 61.0 all-reduce.7
  280.9 49.0 all-gather.19
  332.2 46.8 all-gather.17
  381.3 50.9 all-gather.21
  441.8 63.8 all-reduce.9
  522.9 140.2 reduce-scatter.13
  666.8 72.2 reduce-scatter.27
  742.2 72.2 reduce-scatter.17
  818.1 72.3 reduce-scatter.15
  893.5 71.6 reduce-scatter.19
  968.5 71.7 reduce-scatter.21
  1043.2 64.7 all-reduce.11
  1111.1 75.8 reduce-scatter.29
  1190.2 75.1 reduce-scatter.25
  1268.7 75.1 reduce-scatter.23
where the time goes:
time: 1360 us; the launch traced here: 1350 us
  waiting for transfers between devices  1110 us (82%)
  blocking collectives  103 us (8%)
  matrix products  63.3 us (5%)
  other arithmetic  30.4 us (2%)
  local copies, waits for them, and re-layouts  29.1 us (2%)
  between operations  17.8 us (1%)
    reduce_scatter x1, waiting for transfers between devices, per_device(): lax.psum_scatter(kv_buffer.astype(jnp.bfloat16), 'seq', scatter_dimension...  130 us
    unnamed x21, waiting for transfers between devices  82.5 us
    reduce_scatter x1, waiting for transfers between devices, per_device(): lax.psum_scatter(rows_product(h_norm, grad_gate).astype(jnp.bfloat16), 's...  76.8 us
    reduce_scatter x1, waiting for transfers between devices, per_device(): lax.psum_scatter(rows_product(h_norm, grad_up).astype(jnp.bfloat16), 'seq...  76.5 us
    reduce_scatter x1, waiting for transfers between devices, per_device(): lax.psum_scatter(rows_product(x_norm, grad_query).astype(jnp.bfloat16), '...  74.4 us
    reduce_scatter x1, waiting for transfers between devices, per_device(): lax.psum_scatter(rows_product(x_norm, grad_value).astype(jnp.bfloat16), '...  73.8 us
    reduce_scatter x1, waiting for transfers between devices, per_device(): lax.psum_scatter(rows_product(x_norm, grad_gate_attn).astype(jnp.bfloat16...  73.8 us
    reduce_scatter x1, waiting for transfers between devices, per_device(): lax.psum_scatter(rows_product(x_norm, grad_key).astype(jnp.bfloat16), 'se...  73.2 us
  transfers between devices with their start and end apart: 19, of which 18 were waited for; matrix products, arithmetic and copies ran while one was open for 6% of the time, Pallas kernels for 0%

commit v1 on v0

v1 whole, which is shorter than its diff:
```python
import functools

import jax
import jax.numpy as jnp
from jax import lax
from jax.experimental import pallas as pl
from jax.experimental.pallas import tpu as pltpu
from jax.sharding import PartitionSpec as P

F32 = jnp.float32
BF16 = jnp.bfloat16
MESH = pl.DeviceIdType.MESH
EPS = 1e-06
HEAD = 128
SCALE = HEAD**-0.5
LOG2E = 1.4426950408889634
MASKED = -1e30
FLOOR = -1e29
ROWS = 32


def nn(left, right):
    return jnp.dot(left, right, preferred_element_type=F32)


def nt(left, right):
    return lax.dot_general(left, right, (((1,), (1,)), ((), ())), preferred_element_type=F32)


class Net:
    def __init__(self, send, recv):
        s, k = lax.axis_index("seq"), lax.axis_index("kv")
        self.s, self.k = s, k
        self.x, self.z, self.y, self.c = s // 4, s % 4, k // 2, k % 2
        self.send, self.recv, self.used = send, recv, 0

    def at(self, dx=0, dz=0, dy=0, dc=0):
        return {
            "kv": ((self.y + dy) % 4) * 2 + (self.c + dc) % 2,
            "seq": ((self.x + dx) % 4) * 4 + (self.z + dz) % 4,
        }

    def along(self, axis, d):
        return self.at(dx=d) if axis == 0 else self.at(dz=d)

    def copy(self, src, dst, to):
        i = self.used
        self.used += 1
        return pltpu.make_async_remote_copy(
            src_ref=src,
            dst_ref=dst,
            send_sem=self.send.at[i],
            recv_sem=self.recv.at[i],
            device_id=to,
            device_id_type=MESH,
        )

    def barrier(self):
        sem = pltpu.get_barrier_semaphore()
        near = [self.at(dx=d) for d in (1, 2, 3)] + [self.at(dz=d) for d in (1, 2, 3)]
        near += [self.at(dy=d) for d in (1, 2, 3)] + [self.at(dc=1)]
        for to in near:
            pl.semaphore_signal(sem, inc=1, device_id=to, device_id_type=MESH)
        pl.semaphore_wait(sem, len(near))


class Gather:
    def __init__(self, net, w, cuts):
        q, h, q2, r = cuts
        x, z = net.x, net.z
        place = (x, z)
        self.steps = [[], [], [], []]
        for o, (r0, r1, r2) in enumerate(((0, q, h), (h, q2, r))):
            full, one, two = pl.ds(r0, r2 - r0), pl.ds(r0, r1 - r0), pl.ds(r1, r2 - r1)
            me, other = place[o], place[1 - o]
            low, high = (me + 3) % 4, (me + 1) % 4
            up, down = net.along(o, 1), net.along(o, -1)

            def single(a, rows, o=o, other=other):
                return w.at[a, other, rows] if o == 0 else w.at[other, a, rows]

            def bundle(b, rows, o=o):
                return w.at[:, b, rows] if o == 0 else w.at[b, :, rows]

            def mk(ref, to):
                return net.copy(ref, ref, to)

            self.steps[0] += [mk(single(me, full), up), mk(single(me, full), down)]
            self.steps[1] += [mk(single(low, one), up), mk(single(high, two), down)]
            low, high = (other + 3) % 4, (other + 1) % 4
            up, down = net.along(1 - o, 1), net.along(1 - o, -1)
            self.steps[2] += [mk(bundle(other, full), up), mk(bundle(other, full), down)]
            self.steps[3] += [mk(bundle(low, one), up), mk(bundle(high, two), down)]

    def start(self):
        for d in self.steps[0]:
            d.start()

    def step(self, n):
        if n == 1 or n == 3:
            for a, b in zip(self.steps[n - 1], self.steps[n]):
                a.wait_recv()
                b.start()
        else:
            for o in (0, 1):
                for b in self.steps[1][2 * o : 2 * o + 2]:
                    b.wait_recv()
                for b in self.steps[2][2 * o : 2 * o + 2]:
                    b.start()

    def finish(self):
        for d in self.steps[3]:
            d.wait_recv()

    def drain(self):
        for step in self.steps:
            for d in step:
                d.wait_send()


class Scatter:
    def __init__(self, net, p, rows, bufs):
        self.net, self.p, self.bufs = net, p, bufs
        self.h, self.q = rows // 2, rows // 4
        self.sent = []
        self.d = [{}, {}]

    def rows(self, o, part):
        base = o * self.h
        if part == 1:
            return pl.ds(base, self.q)
        if part == 2:
            return pl.ds(base + self.q, self.q)
        return pl.ds(base, self.h)

    def place(self, o):
        return (self.net.x, self.net.z) if o == 0 else (self.net.z, self.net.x)

    def bundle(self, o, a, part):
        r = self.rows(o, part)
        return self.p.at[a, :, r] if o == 0 else self.p.at[:, a, r]

    def block(self, o, a, i, part):
        r = self.rows(o, part)
        return self.p.at[a, i, r] if o == 0 else self.p.at[i, a, r]

    def go(self, o, name, src, dst, axis, d):
        c = self.net.copy(src, dst, self.net.along(axis, d))
        c.start()
        self.d[o][name] = c
        self.sent.append(c)

    def start(self):
        r1, r2 = self.bufs[0], self.bufs[1]
        q = self.q
        for o in (0, 1):
            me, _ = self.place(o)
            self.go(o, "c1", self.bundle(o, (me + 2) % 4, 1), r1.at[o, 0], o, 1)
            self.go(o, "c2", self.bundle(o, (me + 2) % 4, 2), r1.at[o, 1], o, -1)
        for o in (0, 1):
            me, _ = self.place(o)
            self.go(o, "c3", self.bundle(o, (me + 1) % 4, 2), r2.at[o, 0, :, pl.ds(q, q)], o, 1)
            self.go(o, "c4", self.bundle(o, (me + 3) % 4, 1), r2.at[o, 1, :, pl.ds(0, q)], o, -1)

    def step2(self):
        r1, r2 = self.bufs[0], self.bufs[1]
        q = self.q
        for o in (0, 1):
            me, _ = self.place(o)
            for name, a, part, side, d in (("c1", (me + 1) % 4, 1, 0, 1), ("c2", (me + 3) % 4, 2, 1, -1)):
                self.d[o][name].wait_recv()

                def add(i, _, o=o, a=a, part=part, side=side):
                    b = self.block(o, a, i, part)
                    b[...] = (b[...].astype(F32) + r1[o, side, i].astype(F32)).astype(BF16)
                    return 0

                lax.fori_loop(0, 4, add, 0)
                self.go(o, "c5" if side == 0 else "c6", self.bundle(o, a, part), r2.at[o, side, :, pl.ds(side * q, q)], o, d)

    def step3(self):
        r2, r3, r4 = self.bufs[1], self.bufs[2], self.bufs[3]
        q = self.q
        for o in (0, 1):
            me, other = self.place(o)
            for name in ("c3", "c4", "c5", "c6"):
                self.d[o][name].wait_recv()

            def add(i, o=o, me=me):
                b = self.block(o, me, i, 0)
                total = b[...].astype(F32) + r2[o, 0, i].astype(F32) + r2[o, 1, i].astype(F32)
                b[...] = total.astype(BF16)

            def far(n, _, add=add, other=other):
                add((other + 2 + n) % 4)
                return 0

            add((other + 2) % 4)
            self.go(o, "d1", self.block(o, me, (other + 2) % 4, 1), r3.at[o, 0], 1 - o, 1)
            self.go(o, "d2", self.block(o, me, (other + 2) % 4, 2), r3.at[o, 1], 1 - o, -1)
            lax.fori_loop(1, 4, far, 0)
            self.go(o, "d3", self.block(o, me, (other + 1) % 4, 2), r4.at[o, 0, pl.ds(q, q)], 1 - o, 1)
            self.go(o, "d4", self.block(o, me, (other + 3) % 4, 1), r4.at[o, 1, pl.ds(0, q)], 1 - o, -1)

    def step4(self):
        r3, r4 = self.bufs[2], self.bufs[3]
        q = self.q
        for o in (0, 1):
            me, other = self.place(o)
            for name, a, part, side, d in (("d1", (other + 1) % 4, 1, 0, 1), ("d2", (other + 3) % 4, 2, 1, -1)):
                self.d[o][name].wait_recv()
                b = self.block(o, me, a, part)
                b[...] = (b[...].astype(F32) + r3[o, side].astype(F32)).astype(BF16)
                self.go(o, "d5" if side == 0 else "d6", b, r4.at[o, side, pl.ds(side * q, q)], 1 - o, d)

    def finish(self, store):
        r4 = self.bufs[3]
        for o in (0, 1):
            me, other = self.place(o)
            for name in ("d3", "d4", "d5", "d6"):
                self.d[o][name].wait_recv()
            total = self.block(o, me, other, 0)[...].astype(F32) + r4[o, 0].astype(F32) + r4[o, 1].astype(F32)
            store(self.rows(o, 0), total)

    def drain(self):
        for c in self.sent:
            c.wait_send()


def scatter_bufs(rows, cols):
    h, q = rows // 2, rows // 4
    return [
        pltpu.VMEM((2, 2, 4, q, cols), BF16),
        pltpu.VMEM((2, 2, 4, h, cols), BF16),
        pltpu.VMEM((2, 2, q, cols), BF16),
        pltpu.VMEM((2, 2, h, cols), BF16),
    ]


class ReduceY:
    def __init__(self, net, part, cr, yr):
        self.net, self.part, self.cr, self.yr = net, part, cr, yr

    def start(self):
        n = self.net
        self.core = n.copy(self.part.at[:, 1 - n.c], self.cr, n.at(dc=1))
        self.core.start()

    def step(self):
        n = self.net
        self.core.wait_recv()
        self.far = []
        for d in (2, 1, 3):
            to = (n.y + d) % 4
            own = self.part.at[to, n.c]
            own[...] = (own[...].astype(F32) + self.cr[to].astype(F32)).astype(BF16)
            c = n.copy(own, self.yr.at[d - 1], n.at(dy=d))
            c.start()
            self.far.append(c)

    def finish(self):
        n = self.net
        total = self.part[n.y, n.c].astype(F32) + self.cr[n.y].astype(F32)
        for c in self.far:
            c.wait_recv()
        return total + self.yr[0].astype(F32) + self.yr[1].astype(F32) + self.yr[2].astype(F32)

    def drain(self):
        for c in [self.core] + self.far:
            c.wait_send()


class GatherY:
    def __init__(self, net, g):
        self.net, self.g = net, g

    def start(self):
        n, g = self.net, self.g
        own = g.at[n.y, n.c]
        self.far = [n.copy(own, own, n.at(dy=d)) for d in (1, 2, 3)]
        self.near = [n.copy(own, own, n.at(dc=1))]
        for c in self.far + self.near:
            c.start()

    def step(self):
        n, g = self.net, self.g
        for d, c in zip((1, 2, 3), self.far):
            c.wait_recv()
            came = g.at[(n.y + 4 - d) % 4, n.c]
            on = n.copy(came, came, n.at(dc=1))
            on.start()
            self.near.append(on)

    def finish(self):
        for c in self.near:
            c.wait_recv()

    def drain(self):
        for c in self.far + self.near:
            c.wait_send()


def kernel(*refs):
    it = iter(refs)
    (x_in, cot_in, seg_a, seg_b, gains, wq_in, wg_in, wk_in, wv_in, wo_in, mg_in, mu_in, md_in) = (next(it) for _ in range(13))
    (bo, ig_out, gain1_out, qg_out, gg_out, kg_out, vg_out, og_out, gain2_out, mg_out, mu_out, md_out) = (next(it) for _ in range(12))
    (wqg, wkv, wo, wm, wd, kv, kvg) = (next(it) for _ in range(7))
    (xb, xn, xnt, g, hnb, hnt, dcb, igb) = (next(it) for _ in range(8))
    (part_a, part_b) = (next(it) for _ in range(2))
    yb = [tuple(next(it) for _ in range(2)) for _ in range(4)]
    (r1c, gp, ob, ot, qt, dot_, dqt, dmb, dadu, mt) = (next(it) for _ in range(10))
    (h32, z32, r32, dh32) = (next(it) for _ in range(4))
    (gx0, gxr, gx1, gzr, gy, gc) = (next(it) for _ in range(6))
    sb = [[next(it) for _ in range(4)] for _ in range(6)]
    send, recv, local = (next(it) for _ in range(3))

    net = Net(send, recv)
    s, x, z, y, c = net.s, net.x, net.z, net.y, net.c
    loads = []

    def load(src, dst):
        d = pltpu.make_async_copy(src, dst, local.at[len(loads)])
        d.start()
        loads.append(d)

    load(wo_in, wo.at[x, z, pl.ds(0, 256)])
    load(wq_in, wqg.at[x, z, :, pl.ds(0, 256)])
    load(wg_in, wqg.at[x, z, :, pl.ds(256, 256)])
    load(wk_in, wkv.at[x, z, :, pl.ds(0, 128)])
    load(wv_in, wkv.at[x, z, :, pl.ds(128, 128)])
    load(x_in, xb)
    load(md_in, wd.at[x, z])
    load(mg_in, wm.at[x, z, :, pl.ds(0, 768)])
    load(mu_in, wm.at[x, z, :, pl.ds(768, 768)])
    load(cot_in, g)
    line = lax.broadcasted_iota(jnp.int32, (16, 128), 0)
    tile = jnp.where(line == 0, gains[0:1, :].astype(F32), jnp.where(line == 1, gains[1:2, :].astype(F32), 0.0))
    wo[x, z, 256:272, :] = tile.astype(BF16)
    net.barrier()

    ag_o = Gather(net, wo, (64, 128, 208, 272))
    ag_qg = Gather(net, wqg, (32, 64, 96, 128))
    ag_kvw = Gather(net, wkv, (32, 64, 96, 128))
    ag_kv = Gather(net, kv, (64, 128, 192, 256))
    ag_d = Gather(net, wd, (192, 384, 576, 768))
    ag_m = Gather(net, wm, (32, 64, 96, 128))
    first = (ag_o, ag_qg, ag_kvw)
    for d in loads[:5]:
        d.wait()
    for a in first:
        a.start()

    loads[5].wait()

    def scales(i, _):
        rows = pl.ds(pl.multiple_of(i * 32, 32), 32)
        v = xb[rows, :].astype(F32)
        scale = lax.rsqrt(jnp.mean(v * v, axis=-1, keepdims=True) + EPS)
        r1c[rows, :] = jnp.broadcast_to(scale, (32, 128))
        return 0

    lax.fori_loop(0, 8, scales, 0)
    ids = seg_a[...].astype(F32)

    def below(v):
        return jnp.sum(jnp.where(ids < v, 1.0, 0.0), axis=(0, 1), keepdims=True)

    own_ids = seg_b[pl.ds(s, 1), :].astype(F32)
    first_key = jnp.where(own_ids > 2.5, below(2.5), jnp.where(own_ids > 1.5, below(1.5), jnp.where(own_ids > 0.5, below(0.5), 0.0)))
    first_key = jnp.concatenate([first_key, first_key], axis=1).astype(jnp.int32)
    query_place = s * 256 + lax.broadcasted_iota(jnp.int32, (1, 256), 1)
    query_place = jnp.concatenate([query_place, query_place], axis=1)
    top = jnp.max(ids, axis=(0, 1), keepdims=True)
    kept = below(top)

    for a in first:
        a.step(1)
    for d in loads[6:]:
        d.wait()

    def mask_cot(i, _):
        rows = pl.ds(pl.multiple_of(i * 32, 32), 32)
        place = (s * 256 + i * 32 + lax.broadcasted_iota(jnp.int32, (32, 1), 0)).astype(F32)
        g[rows, :] = jnp.where(place < kept, g[rows, :].astype(F32), 0.0).astype(BF16)
        return 0

    lax.fori_loop(0, 8, mask_cot, 0)

    def clear(j, _):
        kvg[j // 4, j % 4] = jnp.zeros((256, 256), BF16)
        return 0

    lax.fori_loop(s + 1, 16, clear, 0)
    for a in first:
        a.step(2)
    for a in first:
        a.step(3)
    ag_d.start()
    ag_o.finish()

    def gain_row(n):
        return jnp.concatenate([wo[j // 4, j % 4, 256:272, :].astype(F32)[n : n + 1, :] for j in range(16)], axis=1)

    gain1 = gain_row(0)

    def norm_in(i, _):
        rows = pl.ds(pl.multiple_of(i * 32, 32), 32)
        v = xb[rows, :].astype(F32) * r1c[rows, 0:1]
        xn[rows, :] = (v * gain1).astype(BF16)
        return 0

    lax.fori_loop(0, 8, norm_in, 0)
    ag_d.step(1)
    ag_kvw.finish()
    kv[x, z] = nn(xn[...], wkv[...].reshape(2048, 256)).astype(BF16)
    ag_kv.start()
    ag_qg.finish()
    qg = nn(xn[...], wqg[...].reshape(2048, 512))
    q = qg[:, :256].astype(BF16)
    gp[...] = qg[:, 256:]
    qt[...] = jnp.concatenate([q[:, :128].T, q[:, 128:].T], axis=1)
    ag_kv.step(1)
    ag_m.start()
    ag_kv.step(2)
    ag_kv.step(3)
    ag_d.step(2)
    ag_m.step(1)
    ag_kv.finish()

    ot[...] = jnp.zeros_like(ot)
    key_line = lax.broadcasted_iota(jnp.int32, (256, 512), 0)

    def scores(j):
        keys = kv[j // 4, j % 4, :, 0:128]
        values = kv[j // 4, j % 4, :, 128:256]
        place = j * 256 + key_line
        allowed = (place >= first_key) & (place <= query_place)
        return keys, values, jnp.where(allowed, nn(keys, qt[...]) * (SCALE * LOG2E), MASKED)

    def attend(j, state):
        top, total = state
        _, values, st = scores(j)
        new_top = jnp.maximum(top, jnp.max(st, axis=0, keepdims=True))
        probs = jnp.exp2(st - new_top)
        shrink = jnp.exp2(top - new_top)
        ot[...] = ot[...] * shrink + nn(values.T, probs.astype(BF16))
        return new_top, total * shrink + jnp.sum(probs, axis=0, keepdims=True)

    state = (jnp.full((1, 512), FLOOR, F32), jnp.zeros((1, 512), F32))
    top, total = lax.fori_loop(0, s + 1, attend, state)
    lse = top + jnp.log(total) * LOG2E
    ot[...] = ot[...] / total
    o = jnp.concatenate([ot[:, 0:256].T, ot[:, 256:512].T], axis=1)
    ob[...] = o
    yv = (o * jax.nn.sigmoid(gp[...])).astype(BF16)
    ag_m.step(2)
    ag_d.step(3)
    for j in range(8):
        w2 = jnp.concatenate([wo[j // 2, 2 * (j % 2) + i, 0:256, :] for i in (0, 1)], axis=1)
        part_a[:, :, :, 256 * j : 256 * j + 256] = nn(yv, w2).astype(BF16).reshape(4, 2, 32, 256)
    red = ReduceY(net, part_a, *yb[0])
    red.start()
    yt = yv.T
    gain2 = gain_row(1)
    red.step()
    own_rows = pl.ds(pl.multiple_of(net.k * ROWS, ROWS), ROWS)
    h = xb[own_rows, :].astype(F32) + red.finish()
    h32[...] = h
    scale2 = lax.rsqrt(jnp.mean(h * h, axis=-1, keepdims=True) + EPS)
    z2 = h * scale2
    z32[...] = z2
    r32[...] = jnp.broadcast_to(scale2, (ROWS, 128))
    hnb[y, c] = (z2 * gain2).astype(BF16)
    gat = GatherY(net, hnb)
    gat.start()
    ag_m.step(3)
    gat.step()
    ag_d.finish()

    for n in range(3):
        w2 = jnp.concatenate([wd[j // 4, j % 4, 256 * n : 256 * n + 256, :] for j in range(16)], axis=1)
        dmb[:, 256 * n : 256 * n + 256] = nt(g[...], w2)
    gat.finish()
    hn = hnb[...].reshape(256, 2048)
    for j in range(8):
        hnt[256 * j : 256 * j + 256, :] = hnb[:, :, :, 256 * j : 256 * j + 256].reshape(256, 256).T
    ag_m.finish()
    for n in range(3):
        cols = slice(256 * n, 256 * n + 256)
        up_cols = slice(768 + 256 * n, 1024 + 256 * n)
        a = nn(hn, wm[:, :, :, cols].reshape(2048, 256))
        u = nn(hn, wm[:, :, :, up_cols].reshape(2048, 256))
        sig = jax.nn.sigmoid(a)
        silu = a * sig
        mt[cols, :] = (silu * u).astype(BF16).T
        dm = dmb[:, cols]
        dadu[:, cols] = (dm * u * sig * (1.0 + a * (1.0 - sig))).astype(BF16)
        dadu[:, up_cols] = (dm * silu).astype(BF16)
    for a in first + (ag_d, ag_m):
        a.drain()
    red.drain()
    for j in range(8):
        w2 = wm[j // 2, 2 * (j % 2) : 2 * (j % 2) + 2].reshape(256, 1536)
        part_a[:, :, :, 256 * j : 256 * j + 256] = nt(dadu[...], w2).astype(BF16).reshape(4, 2, 32, 256)
    red3 = ReduceY(net, part_a, *yb[1])
    red3.start()
    for j in range(8):
        pm = nn(hnt[256 * j : 256 * j + 256, :], dadu[...])
        wm[j // 2, 2 * (j % 2) : 2 * (j % 2) + 2] = pm.astype(BF16).reshape(2, 128, 1536)
    red3.step()
    rs_m = Scatter(net, wm, 128, sb[0])
    rs_m.start()
    mm = mt[...].T
    for j in range(8):
        w2 = jnp.concatenate([wd[j // 2, 2 * (j % 2) + i] for i in (0, 1)], axis=1)
        part_b[:, :, :, 256 * j : 256 * j + 256] = nn(mm, w2).astype(BF16).reshape(4, 2, 32, 256)
    dhn = red3.finish()
    z2 = z32[...]
    e2 = dhn * gain2
    grads_gain2 = jnp.sum(dhn * z2, axis=0, keepdims=True)
    dh = g[own_rows, :].astype(F32) + r32[:, 0:1] * (e2 - z2 * jnp.mean(e2 * z2, axis=-1, keepdims=True))
    dh32[...] = dh
    dcb[y, c] = dh.astype(BF16)
    gat3 = GatherY(net, dcb)
    gat3.start()
    red2 = ReduceY(net, part_b, *yb[2])
    red2.start()
    for j in range(8):
        pd = nn(mt[...], g[:, 256 * j : 256 * j + 256])
        for i in (0, 1):
            wd[j // 2, 2 * (j % 2) + i] = pd[:, 128 * i : 128 * i + 128].astype(BF16)
    rs_d = Scatter(net, wd, 768, sb[1])
    rs_d.start()
    gat3.step()
    rs_m.step2()
    gat3.finish()
    dc = dcb[...].reshape(256, 2048)
    w2 = jnp.concatenate([wo[j // 4, j % 4, 0:256, :] for j in range(16)], axis=1)
    dy = nt(dc, w2)
    sig = jax.nn.sigmoid(gp[...])
    do = (dy * sig).astype(BF16)
    dg = (dy * ob[...] * sig * (1.0 - sig)).astype(BF16)
    for j in range(8):
        po = nn(yt, dcb[:, :, :, 256 * j : 256 * j + 256].reshape(256, 256))
        for i in (0, 1):
            wo[j // 2, 2 * (j % 2) + i, 0:256, :] = po[:, 128 * i : 128 * i + 128].astype(BF16)
    dot_[...] = jnp.concatenate([do[:, :128].T, do[:, 128:].T], axis=1)
    q_rows = jnp.concatenate([qt[:, 0:256].T, qt[:, 256:512].T], axis=0)
    do_rows = jnp.concatenate([do[:, :128], do[:, 128:]], axis=0)
    w = jnp.sum(dot_[...].astype(F32) * ot[...], axis=0, keepdims=True)
    red2.step()
    rs_d.step2()
    rs_m.step3()
    dqt[...] = jnp.zeros_like(dqt)

    def attend_back(j, _):
        keys, values, st = scores(j)
        probs = jnp.exp2(st - lse)
        dp = nn(values, dot_[...])
        ds = (probs * (dp - w) * SCALE).astype(BF16)
        kvg[j // 4, j % 4, :, 0:128] = nn(ds, q_rows).astype(BF16)
        kvg[j // 4, j % 4, :, 128:256] = nn(probs.astype(BF16), do_rows).astype(BF16)
        dqt[...] += nn(keys.T, ds)
        return 0

    lax.fori_loop(0, s + 1, attend_back, 0)
    rs_kv = Scatter(net, kvg, 256, sb[2])
    rs_kv.start()
    rs_d.step3()
    rs_m.step4()
    dq = jnp.concatenate([dqt[:, 0:256].T, dqt[:, 256:512].T], axis=1).astype(BF16)
    dqdg = jnp.concatenate([dq, dg], axis=1)
    rs_kv.step2()
    rs_d.step4()
    for j in range(8):
        xnt[256 * j : 256 * j + 256, :] = xn[:, 256 * j : 256 * j + 256].T
    red3.drain()
    rs_kv.step3()
    for j in range(8):
        w2 = wqg[j // 2, 2 * (j % 2) : 2 * (j % 2) + 2].reshape(256, 512)
        xn[:, 256 * j : 256 * j + 256] = nt(dqdg, w2).astype(BF16)
        pq = nn(xnt[256 * j : 256 * j + 256, :], dqdg)
        wqg[j // 2, 2 * (j % 2) : 2 * (j % 2) + 2] = pq.astype(BF16).reshape(2, 128, 512)
    rs_kv.step4()
    rs_qg = Scatter(net, wqg, 128, sb[3])
    rs_qg.start()
    rs_o = Scatter(net, wo, 256, sb[4])
    rs_o.start()

    def store_kv(rows, v):
        kv[0, 0, rows, :] = v.astype(BF16)

    ag_kv.drain()
    rs_kv.finish(store_kv)
    dkdv = kv[0, 0]
    for j in range(8):
        w2 = wkv[j // 2, 2 * (j % 2) : 2 * (j % 2) + 2].reshape(256, 256)
        px = nt(dkdv, w2) + xn[:, 256 * j : 256 * j + 256].astype(F32)
        part_a[:, :, :, 256 * j : 256 * j + 256] = px.astype(BF16).reshape(4, 2, 32, 256)
    red4 = ReduceY(net, part_a, *yb[3])
    red4.start()
    for j in range(8):
        pk = nn(xnt[256 * j : 256 * j + 256, :], dkdv)
        wkv[j // 2, 2 * (j % 2) : 2 * (j % 2) + 2] = pk.astype(BF16).reshape(2, 128, 256)
    rs_kvw = Scatter(net, wkv, 128, sb[5])
    rs_kvw.start()
    red4.step()
    rs_qg.step2()
    rs_o.step2()
    rs_kvw.step2()
    bo[y, c] = (h32[...] + red2.finish()).astype(BF16)
    gat2 = GatherY(net, bo)
    gat2.start()
    dxn = red4.finish()
    scale1 = r1c[own_rows, 0:1]
    z1 = xb[own_rows, :].astype(F32) * scale1
    e1 = dxn * gain1
    grads_gain1 = jnp.sum(dxn * z1, axis=0, keepdims=True)
    input_grad = dh32[...] + scale1 * (e1 - z1 * jnp.mean(e1 * z1, axis=-1, keepdims=True))
    igb[y, c] = input_grad.astype(BF16)
    gat4 = GatherY(net, igb)
    gat4.start()
    line8 = lax.broadcasted_iota(jnp.int32, (8, 128), 0)
    for j in range(16):
        cols = slice(128 * j, 128 * j + 128)
        gx0[j // 4, j % 4] = jnp.where(line8 == 0, grads_gain1[:, cols], jnp.where(line8 == 1, grads_gain2[:, cols], 0.0))
    cx = [net.copy(gx0.at[(x + d) % 4], gxr.at[d - 1], net.at(dx=d)) for d in (1, 2, 3)]
    for d in cx:
        d.start()
    rs_qg.step3()
    rs_o.step3()
    rs_kvw.step3()
    for d in cx:
        d.wait_recv()
    gx1[...] = gx0[x] + gxr[0] + gxr[1] + gxr[2]
    cz = [net.copy(gx1.at[(z + d) % 4], gzr.at[d - 1], net.at(dz=d)) for d in (1, 2, 3)]
    for d in cz:
        d.start()
    gat2.step()
    gat4.step()
    rs_qg.step4()
    rs_o.step4()
    rs_kvw.step4()
    for d in cz:
        d.wait_recv()
    gy[y] = gx1[z] + gzr[0] + gzr[1] + gzr[2]
    cy = [net.copy(gy.at[y], gy.at[y], net.at(dy=d)) for d in (1, 2, 3)]
    for d in cy:
        d.start()

    def store_m(rows, v):
        mg_out[rows, :] = v[:, :768]
        mu_out[rows, :] = v[:, 768:]

    def store_d(rows, v):
        md_out[rows, :] = v

    rs_m.finish(store_m)
    rs_d.finish(store_d)
    for d in cy:
        d.wait_recv()
    gc[c] = gy[0] + gy[1] + gy[2] + gy[3]
    cc = net.copy(gc.at[c], gc.at[c], net.at(dc=1))
    cc.start()

    def store_qg(rows, v):
        qg_out[rows, :] = v[:, :256]
        gg_out[rows, :] = v[:, 256:]

    def store_kvw(rows, v):
        kg_out[rows, :] = v[:, :128]
        vg_out[rows, :] = v[:, 128:]

    def store_o(rows, v):
        og_out[rows, :] = v

    rs_qg.finish(store_qg)
    rs_o.finish(store_o)
    rs_kvw.finish(store_kvw)
    gat2.finish()
    gat4.finish()

    def widen(i, _):
        ig_out[i // 2, i % 2] = igb[i // 2, i % 2].astype(F32)
        return 0

    lax.fori_loop(0, 8, widen, 0)
    cc.wait_recv()
    sums = gc[0] + gc[1]
    gain1_out[...] = sums[0:1, :]
    gain2_out[...] = sums[1:2, :]
    for a in (rs_m, rs_d, rs_kv, rs_qg, rs_o, rs_kvw, red2, red4, gat, gat2, gat3, gat4):
        a.drain()
    for d in cx + cz + cy + [cc]:
        d.wait_send()


def per_device(inputs, cotangent, segment_ids, attn_gain, query_weight, gate_weight, key_weight, value_weight, output_weight, mlp_gain, mlp_gate, mlp_up, mlp_down):
    v = pltpu.VMEM
    y_rows = (4, 2, ROWS, 2048)
    scratch = [
        v((4, 4, 128, 512), BF16),
        v((4, 4, 128, 256), BF16),
        v((4, 4, 272, 128), BF16),
        v((4, 4, 128, 1536), BF16),
        v((4, 4, 768, 128), BF16),
        v((4, 4, 256, 256), BF16),
        v((4, 4, 256, 256), BF16),
        v((256, 2048), BF16),
        v((256, 2048), BF16),
        v((2048, 256), BF16),
        v((256, 2048), BF16),
        v(y_rows, BF16),
        v((2048, 256), BF16),
        v(y_rows, BF16),
        v(y_rows, BF16),
        v(y_rows, BF16),
        v(y_rows, BF16),
    ]
    for _ in range(4):
        scratch += [v((4, ROWS, 2048), BF16), v((3, ROWS, 2048), BF16)]
    scratch += [
        v((256, 128), F32),
        v((256, 256), F32),
        v((256, 256), F32),
        v((128, 512), F32),
        v((128, 512), BF16),
        v((128, 512), BF16),
        v((128, 512), F32),
        v((256, 768), F32),
        v((256, 1536), BF16),
        v((768, 256), BF16),
        v((ROWS, 2048), F32),
        v((ROWS, 2048), F32),
        v((ROWS, 128), F32),
        v((ROWS, 2048), F32),
        v((4, 4, 8, 128), F32),
        v((3, 4, 8, 128), F32),
        v((4, 8, 128), F32),
        v((3, 8, 128), F32),
        v((4, 8, 128), F32),
        v((2, 8, 128), F32),
    ]
    for rows, cols in ((128, 1536), (768, 128), (256, 256), (128, 512), (256, 128), (128, 256)):
        scratch += scatter_bufs(rows, cols)
    n_sems = 320
    scratch += [pltpu.SemaphoreType.DMA((n_sems,)), pltpu.SemaphoreType.DMA((n_sems,)), pltpu.SemaphoreType.DMA((16,))]
    whole = pl.BlockSpec(memory_space=pltpu.VMEM)
    there = pl.BlockSpec(memory_space=pl.ANY)
    shape = jax.ShapeDtypeStruct
    outs = pl.pallas_call(
        kernel,
        out_shape=(
            shape(y_rows, BF16),
            shape(y_rows, F32),
            shape((1, 128), F32),
            shape((128, 256), F32),
            shape((128, 256), F32),
            shape((128, 128), F32),
            shape((128, 128), F32),
            shape((256, 128), F32),
            shape((1, 128), F32),
            shape((128, 768), F32),
            shape((128, 768), F32),
            shape((768, 128), F32),
        ),
        in_specs=[there, there, whole, whole, whole] + [there] * 8,
        out_specs=[whole] * 12,
        scratch_shapes=scratch,
        compiler_params=pltpu.CompilerParams(collective_id=0, has_side_effects=True, vmem_limit_bytes=63 << 20),
    )(
        inputs,
        cotangent,
        segment_ids.reshape(32, 128),
        segment_ids.reshape(16, 256),
        jnp.stack([attn_gain, mlp_gain]),
        query_weight,
        gate_weight,
        key_weight,
        value_weight,
        output_weight,
        mlp_gate,
        mlp_up,
        mlp_down,
    )
    outs = list(outs)
    outs[0] = outs[0].reshape(256, 2048)
    outs[1] = outs[1].reshape(256, 2048)
    outs[2] = outs[2].reshape(128)
    outs[8] = outs[8].reshape(128)
    return tuple(outs)


def solution(mesh):
    weights = (P("seq"), P("seq", "kv"), P("seq", "kv"), P("seq", "kv"), P("seq", "kv"), P("kv", "seq"))
    weights += (P("seq"), P("seq", "kv"), P("seq", "kv"), P("kv", "seq"))
    return jax.shard_map(
        per_device,
        mesh=mesh,
        in_specs=(P("seq", None), P("seq", None), P()) + weights,
        out_specs=(P("seq", None), P("seq", None)) + weights,
        check_vma=False,
    )
```

time: 1360 us -> 217 us (0.16)
  waiting for transfers between devices: 1110 us -> 0 us
  Pallas kernels: 0 us -> 202 us
  blocking collectives: 103 us -> 0 us
  matrix products: 63.3 us -> 0 us
  other arithmetic: 30.4 us -> 1.19 us
  local copies, waits for them, and re-layouts: 29.1 us -> 11.6 us
  between operations: 17.8 us -> 0.73 us
    reduce_scatter x7 -> x0, waiting for transfers between devices: 578 us -> none  [the longest x1 130 us: per_device(): lax.psum_scatter(kv_buffer.astype(jnp.bfloat16), 'seq', scatter_dimension...]
    all_gather x7 -> x0, waiting for transfers between devices: 273 us -> none  [the longest x1 53.3 us: per_device(): lax.all_gather(jnp.concatenate([key_local, value_local], axis=1), 'seq',...]
    pallas_call x0 -> x1, Pallas kernels: none -> 202 us  [per_device(): pl.pallas_call(kernel, out_shape=(shape(y_rows, BF16), shape(y_rows, F32)...]
    psum x3 -> x0, waiting for transfers between devices: 173 us -> none  [the longest x1 66.2 us: per_device(): lax.psum(jnp.dot(mixed, w_down, preferred_element_type=jnp.float32).astyp...]
    unnamed x21 -> x0, waiting for transfers between devices: 82.5 us -> none
    all_gather x4 -> x0, blocking collectives: 69.2 us -> none  [the longest x1 18.3 us: per_device(): lax.all_gather(attn_gain, 'seq', axis=0, tiled=True)]
    dot_general x33 -> x0, matrix products: 63.3 us -> none  [the longest x8 20.1 us: rows_product(): lax.dot_general(left, right, (((0,), (0,)), ((), ())), preferred_element_...]
    unnamed x1 -> x0, blocking collectives: 34 us -> none
  transfers between devices with their start and end apart: 19 -> 0, of which waited for: 18 -> 0; matrix products, arithmetic and copies ran while one was open for 6% -> 0% of each run, Pallas kernels for 0% -> 0%
where the time goes in v1:
time: 217 us; the launch traced here: 216 us
  Pallas kernels  202 us (93%)
  local copies, waits for them, and re-layouts  11.6 us (5%)
    pallas_call x1, Pallas kernels, per_device(): pl.pallas_call(kernel, out_shape=(shape(y_rows, BF16), shape(y_rows, F32)...  202 us
    unnamed x34, local copies, waits for them, and re-layouts  10.3 us

profile of v1, /device:TPU:1, one launch (start us, length us, event | category | flops | bytes accessed | tf_op | source)
XLA Modules:
  0.0 215.7 jit_solution(12344625464090928561)
XLA Ops:
  0.6 1.2 pad_maximum_fusion.refs_4_
  1.8 1.3 reshape.43.refs_3_
  3.2 202.2 %shard_map.220 = (bf16[4,2,32,2048]{3,2,1,0:T(8,128)(2,1)}, f32[4,2,32,2048]{3,2,1,0:T(8,128)}, f32[1,128]{1,0:T(1,128)}, f32[128,256]{1,0:T(8,128)}, f32[128,25...) custom-call(bf16[256,2048]{1,0:T(8,128)(2,1)} %refs_0_.1, ...), custom_call_target="tpu_custom_call" | custom-call | tf_op jit(solution)/shard_map/pallas_call | solution.py:751
  205.4 0.0 copy-start
  205.4 2.5 %copy.37 = bf16[256,2048]{1,0:T(8,128)(2,1)} copy(bf16[256,2048]{1,0:T(8,128)(2,1)} %bitcast.8) | data formatting | bytes 2097152
  207.8 0.0 copy-done
  207.8 0.0 copy-start.10
  207.8 0.0 copy-start.6
  207.8 0.0 copy-start.5
  207.8 0.0 copy-start.8
  207.8 0.0 copy-start.7
  207.8 0.0 copy-start.4
  207.9 0.0 copy-start.9
  207.9 0.0 copy-start.3
  207.9 0.0 copy-start.2
  207.9 1.3 copy.38
  209.2 0.0 copy-done.10
  209.2 0.0 copy-start.1
  209.2 0.5 copy.39
  209.7 0.0 copy-done.6
  209.7 0.7 copy.40
  210.4 0.0 copy-done.5
  210.4 0.7 copy.41
  211.0 0.0 copy-done.8
  211.0 0.6 copy.42
  211.7 0.0 copy-done.7
  211.7 0.6 copy.43
  212.3 0.0 copy-done.4
  212.3 0.7 copy.44
  213.0 0.0 copy-done.9
  213.0 0.5 copy.45
  213.5 0.0 copy-done.3
  213.5 0.7 copy.46
  214.2 0.0 copy-done.2
  214.2 0.7 copy.47
  215.0 0.0 copy-done.1
  215.0 0.7 copy.48
Async XLA Ops:
  205.4 2.5 %copy-start = (f32[4,2,32,2048]{3,2,1,0:T(8,128)S(1)}, f32[4,2,32,2048]{3,2,1,0:T(8,128)}, u32[]{:S(2)}) copy-start(f32[4,2,32,2048]{3,2,1,0:T(8,128)} %get-tuple-element.25) | copy-start | bytes 6291460
  207.8 1.4 copy-start.10
  207.8 1.9 copy-start.6
  207.8 2.6 %copy-start.5 = (f32[128,256]{1,0:T(8,128)S(1)}, f32[128,256]{1,0:T(8,128)}, u32[]{:S(2)}) copy-start(f32[128,256]{1,0:T(8,128)} %get-tuple-element.52) | copy-start | bytes 393220
  207.8 3.2 %copy-start.8 = (f32[128,128]{1,0:T(8,128)S(1)}, f32[128,128]{1,0:T(8,128)}, u32[]{:S(2)}) copy-start(f32[128,128]{1,0:T(8,128)} %get-tuple-element.53) | copy-start | bytes 196612
  207.8 3.8 %copy-start.7 = (f32[128,128]{1,0:T(8,128)S(1)}, f32[128,128]{1,0:T(8,128)}, u32[]{:S(2)}) copy-start(f32[128,128]{1,0:T(8,128)} %get-tuple-element.54) | copy-start | bytes 196612
  207.8 4.5 %copy-start.4 = (f32[256,128]{1,0:T(8,128)S(1)}, f32[256,128]{1,0:T(8,128)}, u32[]{:S(2)}) copy-start(f32[256,128]{1,0:T(8,128)} %get-tuple-element.55) | copy-start | bytes 393220
  207.9 5.1 %copy-start.9 = (f32[1,128]{1,0:T(1,128)S(1)}, f32[1,128]{1,0:T(1,128)}, u32[]{:S(2)}) copy-start(f32[1,128]{1,0:T(1,128)} %get-tuple-element.32) | copy-start | bytes 1540
  207.9 5.6 %copy-start.3 = (f32[128,768]{1,0:T(8,128)S(1)}, f32[128,768]{1,0:T(8,128)}, u32[]{:S(2)}) copy-start(f32[128,768]{1,0:T(8,128)} %get-tuple-element.57) | copy-start | bytes 1179652
  207.9 6.4 %copy-start.2 = (f32[128,768]{1,0:T(8,128)S(1)}, f32[128,768]{1,0:T(8,128)}, u32[]{:S(2)}) copy-start(f32[128,768]{1,0:T(8,128)} %get-tuple-element.58) | copy-start | bytes 1179652
  209.2 5.8 %copy-start.1 = (f32[768,128]{1,0:T(8,128)S(1)}, f32[768,128]{1,0:T(8,128)}, u32[]{:S(2)}) copy-start(f32[768,128]{1,0:T(8,128)} %get-tuple-element.59) | copy-start | bytes 1179652

commit v2 on v1

v2 whole, which is shorter than its diff:
```python
import functools

import jax
import jax.numpy as jnp
from jax import lax
from jax.experimental import pallas as pl
from jax.experimental.pallas import tpu as pltpu
from jax.sharding import PartitionSpec as P

F32 = jnp.float32
BF16 = jnp.bfloat16
MESH = pl.DeviceIdType.MESH
EPS = 1e-06
HEAD = 128
SCALE = HEAD**-0.5
LOG2E = 1.4426950408889634
MASKED = -1e30
FLOOR = -1e29
ROWS = 32


def nn(left, right):
    return jnp.dot(left, right, preferred_element_type=F32)


def nt(left, right):
    return lax.dot_general(left, right, (((1,), (1,)), ((), ())), preferred_element_type=F32)


class Net:
    def __init__(self, sems):
        s, k = lax.axis_index("seq"), lax.axis_index("kv")
        self.s, self.k = s, k
        self.x, self.z, self.y, self.c = s // 4, s % 4, k // 2, k % 2
        self.sems, self.used = sems, 0

    def at(self, dx=0, dz=0, dy=0, dc=0):
        return {
            "kv": ((self.y + dy) % 4) * 2 + (self.c + dc) % 2,
            "seq": ((self.x + dx) % 4) * 4 + (self.z + dz) % 4,
        }

    def along(self, axis, d):
        return self.at(dx=d) if axis == 0 else self.at(dz=d)

    def sem(self):
        self.used += 1
        return self.sems.at[self.used - 1]

    def copy(self, src, dst, to, sent, came):
        return pltpu.make_async_remote_copy(
            src_ref=src,
            dst_ref=dst,
            send_sem=sent,
            recv_sem=came,
            device_id=to,
            device_id_type=MESH,
        )

    def send(self, src, dst, to, sent, came):
        self.copy(src, dst, to, sent, came).start()

    def wait_sent(self, ref, sem):
        self.copy(ref, ref, self.at(dc=1), sem, sem).wait_send()

    def wait_came(self, ref, sem):
        self.copy(ref, ref, self.at(dc=1), sem, sem).wait_recv()

    def barrier(self):
        sem = pltpu.get_barrier_semaphore()
        near = [self.at(dx=d) for d in (1, 2, 3)] + [self.at(dz=d) for d in (1, 2, 3)]
        near += [self.at(dy=d) for d in (1, 2, 3)] + [self.at(dc=1)]
        for to in near:
            pl.semaphore_signal(sem, inc=1, device_id=to, device_id_type=MESH)
        pl.semaphore_wait(sem, len(near))


class Gather:
    def __init__(self, net, w, cuts, cols=slice(None)):
        self.net, self.w, self.cols = net, w, cols
        q, h, q2, r = cuts
        self.spans = ((0, q, h), (h, q2, r))
        self.rows = pl.ds(0, r)
        self.sent = [net.sem() for _ in range(4)]
        self.came = [[[net.sem(), net.sem()], [net.sem()], [net.sem(), net.sem()], [net.sem()]] for _ in (0, 1)]

    def part(self, o, n):
        r0, r1, r2 = self.spans[o]
        return (pl.ds(r0, r2 - r0), pl.ds(r0, r1 - r0), pl.ds(r1, r2 - r1))[n]

    def single(self, o, a, n):
        x, z = (a, self.net.z) if o == 0 else (self.net.x, a)
        return self.w.at[x, z, self.part(o, n), self.cols]

    def bundle(self, o, b, n):
        rows = self.part(o, n)
        return self.w.at[:, b, rows, self.cols] if o == 0 else self.w.at[b, :, rows, self.cols]

    def push(self, o, n, ref, axis, d, sem):
        self.net.send(ref, ref, self.net.along(axis, d), self.sent[n], sem)

    def start(self):
        for o in (0, 1):
            own = self.single(o, (self.net.x, self.net.z)[o], 0)
            self.push(o, 0, own, o, 1, self.came[o][0][0])
            self.push(o, 0, own, o, -1, self.came[o][0][1])

    def step(self, n):
        net = self.net
        for o in (0, 1):
            me, other = (net.x, net.z) if o == 0 else (net.z, net.x)
            came = self.came[o]
            if n == 1:
                low, high = (me + 3) % 4, (me + 1) % 4
                net.wait_came(self.single(o, low, 0), came[0][0])
                self.push(o, 1, self.single(o, low, 1), o, 1, came[1][0])
                net.wait_came(self.single(o, high, 0), came[0][1])
                self.push(o, 1, self.single(o, high, 2), o, -1, came[1][0])
            elif n == 2:
                net.wait_came(self.single(o, (me + 2) % 4, 0), came[1][0])
                own = self.bundle(o, other, 0)
                self.push(o, 2, own, 1 - o, 1, came[2][0])
                self.push(o, 2, own, 1 - o, -1, came[2][1])
            else:
                low, high = (other + 3) % 4, (other + 1) % 4
                net.wait_came(self.bundle(o, low, 0), came[2][0])
                self.push(o, 3, self.bundle(o, low, 1), 1 - o, 1, came[3][0])
                net.wait_came(self.bundle(o, high, 0), came[2][1])
                self.push(o, 3, self.bundle(o, high, 2), 1 - o, -1, came[3][0])

    def finish(self):
        for o in (0, 1):
            other = self.net.z if o == 0 else self.net.x
            self.net.wait_came(self.bundle(o, (other + 2) % 4, 0), self.came[o][3][0])

    def drain(self):
        w, rows, cols = self.w, self.rows, self.cols
        for ref, sem in zip((w.at[0, 0:2, rows, cols], w.at[0, 0, rows, cols], w.at[0:2, :, rows, cols], w.at[0, :, rows, cols]), self.sent):
            self.net.wait_sent(ref, sem)


class Scatter:
    def __init__(self, net, p, rows, bufs, cols=slice(None)):
        self.net, self.p, self.bufs, self.cols = net, p, bufs, cols
        self.r, self.h, self.q = rows, rows // 2, rows // 4
        self.sent = [net.sem(), net.sem()]
        self.came = [[[net.sem(), net.sem()] for _ in range(4)] for _ in (0, 1)]

    def rows(self, o, part):
        base = o * self.h
        if part == 1:
            return pl.ds(base, self.q)
        if part == 2:
            return pl.ds(base + self.q, self.q)
        return pl.ds(base, self.h)

    def place(self, o):
        return (self.net.x, self.net.z) if o == 0 else (self.net.z, self.net.x)

    def bundle(self, o, a, part):
        r = self.rows(o, part)
        return self.p.at[a, :, r, self.cols] if o == 0 else self.p.at[:, a, r, self.cols]

    def block(self, o, a, i, part):
        r = self.rows(o, part)
        return self.p.at[a, i, r, self.cols] if o == 0 else self.p.at[i, a, r, self.cols]

    def half(self, side):
        return pl.ds(side * self.q, self.q)

    def start(self):
        r1, r2 = self.bufs[0], self.bufs[1]
        for o in (0, 1):
            me, _ = self.place(o)
            for side, d in ((0, 1), (1, -1)):
                self.net.send(self.bundle(o, (me + 2) % 4, 1 + side), r1.at[o, side], self.net.along(o, d), self.sent[0], self.came[o][0][side])
        for o in (0, 1):
            me, _ = self.place(o)
            for side, d in ((0, 1), (1, -1)):
                self.net.send(self.bundle(o, (me + d) % 4, 2 - side), r2.at[o, side, :, self.half(1 - side)], self.net.along(o, d), self.sent[0], self.came[o][1][side])

    def step2(self):
        r1, r2 = self.bufs[0], self.bufs[1]
        for o in (0, 1):
            me, _ = self.place(o)
            for side, d in ((0, 1), (1, -1)):
                a, part = (me + d) % 4, 1 + side
                self.net.wait_came(r1.at[o, side], self.came[o][0][side])

                def add(i, _, o=o, a=a, part=part, side=side):
                    b = self.block(o, a, i, part)
                    b[...] = (b[...].astype(F32) + r1[o, side, i].astype(F32)).astype(BF16)
                    return 0

                lax.fori_loop(0, 4, add, 0)
                self.net.send(self.bundle(o, a, part), r2.at[o, side, :, self.half(side)], self.net.along(o, d), self.sent[0], self.came[o][1][side])

    def step3(self):
        r2, r3, r4 = self.bufs[1], self.bufs[2], self.bufs[3]
        for o in (0, 1):
            me, other = self.place(o)
            for side in (0, 1):
                self.net.wait_came(r2.at[o, side], self.came[o][1][side])

            def add(i, o=o, me=me):
                b = self.block(o, me, i, 0)
                total = b[...].astype(F32) + r2[o, 0, i].astype(F32) + r2[o, 1, i].astype(F32)
                b[...] = total.astype(BF16)

            def far(n, _, add=add, other=other):
                add((other + 2 + n) % 4)
                return 0

            add((other + 2) % 4)
            for side, d in ((0, 1), (1, -1)):
                self.net.send(self.block(o, me, (other + 2) % 4, 1 + side), r3.at[o, side], self.net.along(1 - o, d), self.sent[1], self.came[o][2][side])
            lax.fori_loop(1, 4, far, 0)
            for side, d in ((0, 1), (1, -1)):
                self.net.send(self.block(o, me, (other + d) % 4, 2 - side), r4.at[o, side, self.half(1 - side)], self.net.along(1 - o, d), self.sent[1], self.came[o][3][side])

    def step4(self):
        r3, r4 = self.bufs[2], self.bufs[3]
        for o in (0, 1):
            me, other = self.place(o)
            for side, d in ((0, 1), (1, -1)):
                self.net.wait_came(r3.at[o, side], self.came[o][2][side])
                b = self.block(o, me, (other + d) % 4, 1 + side)
                b[...] = (b[...].astype(F32) + r3[o, side].astype(F32)).astype(BF16)
                self.net.send(b, r4.at[o, side, self.half(side)], self.net.along(1 - o, d), self.sent[1], self.came[o][3][side])

    def finish(self, store):
        r4 = self.bufs[3]
        for o in (0, 1):
            me, other = self.place(o)
            for side in (0, 1):
                self.net.wait_came(r4.at[o, side], self.came[o][3][side])
            total = self.block(o, me, other, 0)[...].astype(F32) + r4[o, 0].astype(F32) + r4[o, 1].astype(F32)
            store(self.rows(o, 0), total)

    def drain(self):
        rows = pl.ds(0, self.r)
        self.net.wait_sent(self.p.at[0:3, :, rows, self.cols], self.sent[0])
        self.net.wait_sent(self.p.at[0, 0:3, rows, self.cols], self.sent[1])


def scatter_bufs(rows, cols):
    h, q = rows // 2, rows // 4
    return [
        pltpu.VMEM((2, 2, 4, q, cols), BF16),
        pltpu.VMEM((2, 2, 4, h, cols), BF16),
        pltpu.VMEM((2, 2, q, cols), BF16),
        pltpu.VMEM((2, 2, h, cols), BF16),
    ]


class ReduceY:
    def __init__(self, net, part, cr, yr):
        self.net, self.part, self.cr, self.yr = net, part, cr, yr
        self.sent, self.came, self.core = [net.sem(), net.sem()], net.sem(), [net.sem(), net.sem()]

    def cols(self, n):
        return pl.ds(1024 * n, 1024)

    def start(self, n):
        net, cols = self.net, self.cols(n)
        net.send(self.part.at[:, 1 - net.c, :, cols], self.cr.at[:, :, cols], net.at(dc=1), self.sent[0], self.core[n])

    def step(self, n):
        net, cols = self.net, self.cols(n)
        net.wait_came(self.cr.at[:, :, cols], self.core[n])
        for d in (2, 1, 3):
            to = (net.y + d) % 4
            own = self.part.at[to, net.c, :, cols]
            own[...] = (own[...].astype(F32) + self.cr[to, :, cols].astype(F32)).astype(BF16)
            net.send(own, self.yr.at[d - 1, :, cols], net.at(dy=d), self.sent[1], self.came)

    def finish(self):
        net = self.net
        total = self.part[net.y, net.c].astype(F32) + self.cr[net.y].astype(F32)
        net.wait_came(self.yr, self.came)
        return total + self.yr[0].astype(F32) + self.yr[1].astype(F32) + self.yr[2].astype(F32)

    def drain(self):
        self.net.wait_sent(self.cr, self.sent[0])
        self.net.wait_sent(self.yr, self.sent[1])


class GatherY:
    def __init__(self, net, g):
        self.net, self.g = net, g
        self.sent, self.near, self.far = [net.sem(), net.sem()], net.sem(), [net.sem() for _ in range(3)]

    def start(self):
        n = self.net
        own = self.g.at[n.y, n.c]
        for d in (1, 2, 3):
            n.send(own, own, n.at(dy=d), self.sent[0], self.far[d - 1])
        n.send(own, own, n.at(dc=1), self.sent[1], self.near)

    def step(self):
        n = self.net
        for d in (1, 3, 2):
            came = self.g.at[(n.y + 4 - d) % 4, n.c]
            n.wait_came(came, self.far[d - 1])
            n.send(came, came, n.at(dc=1), self.sent[1], self.near)

    def finish(self):
        self.net.wait_came(self.g.at[:, 1 - self.net.c], self.near)

    def drain(self):
        self.net.wait_sent(self.g.at[0:3, 0], self.sent[0])
        self.net.wait_sent(self.g.at[:, 0], self.sent[1])


def kernel(*refs):
    it = iter(refs)

    def take(n):
        return [next(it) for _ in range(n)]

    x_in, cot_in, seg, gain_a, gain_b, wq_in, wg_in, wk_in, wv_in, wo_in, mg_in, mu_in, md_in = take(13)
    bo_out, ig_out, gain1_out, qg_out, gg_out, kg_out, vg_out, og_out, gain2_out, mg_out, mu_out, md_out = take(12)
    wq, wg, wkv, wo, wm, wd, kv, kvg = take(8)
    xb, xn, xnt, g, hnb, hnt, dcb, igb, bo = take(9)
    part_a, part_b = take(2)
    yb = [take(2) for _ in range(4)]
    r1c, gp, ob, ot, qt, dot_, dqt, dmb, ab, dadu, mt = take(11)
    h32, z32, r32, dh32 = take(4)
    gx0, gxr, gx1, gzr, gy, gc = take(6)
    mg_f, mu_f, md_f, og_f, qg_f, gg_f, kg_f, vg_f, gn_f = take(9)
    sb = [take(4) for _ in range(8)]
    sems, local = take(2)

    net = Net(sems)
    s, x, z, y, c = net.s, net.x, net.z, net.y, net.c
    moved = []

    def move(src, dst):
        d = pltpu.make_async_copy(src, dst, local.at[len(moved)])
        d.start()
        moved.append(d)
        return d

    load_kv = [move(wk_in, wkv.at[x, z, pl.ds(0, 128), pl.ds(0, 128)]), move(wv_in, wkv.at[x, z, pl.ds(0, 128), pl.ds(128, 128)])]
    load_q = move(wq_in, wq.at[x, z])
    load_g = move(wg_in, wg.at[x, z])
    load_o = move(wo_in, wo.at[x, z])
    load_x = move(x_in, xb)
    load_d = move(md_in, wd.at[x, z])
    load_m = [move(mg_in, wm.at[x, z, :, pl.ds(0, 768)]), move(mu_in, wm.at[x, z, :, pl.ds(768, 768)])]
    load_c = move(cot_in, g)
    line = lax.broadcasted_iota(jnp.int32, (16, 128), 0)
    tile = jnp.where(line == 0, gain_a[...].astype(F32), jnp.where(line == 1, gain_b[...].astype(F32), 0.0))
    wkv[x, z, 128:144, :] = jnp.concatenate([tile, tile], axis=1).astype(BF16)
    net.barrier()

    ag_kvw = Gather(net, wkv, (32, 64, 112, 144))
    ag_q = Gather(net, wq, (32, 64, 96, 128))
    ag_g = Gather(net, wg, (32, 64, 96, 128))
    ag_o = Gather(net, wo, (64, 128, 192, 256))
    ag_kv = Gather(net, kv, (64, 128, 192, 256))
    ag_d = Gather(net, wd, (192, 384, 576, 768))
    ag_mg = Gather(net, wm, (32, 64, 96, 128), pl.ds(0, 768))
    ag_mu = Gather(net, wm, (32, 64, 96, 128), pl.ds(768, 768))
    for d in load_kv:
        d.wait()
    ag_kvw.start()
    load_q.wait()
    ag_q.start()
    load_g.wait()
    ag_g.start()
    load_o.wait()
    ag_o.start()
    load_d.wait()
    ag_d.start()

    load_x.wait()

    def scales(i, _):
        rows = pl.ds(pl.multiple_of(i * 32, 32), 32)
        v = xb[rows, :].astype(F32)
        scale = lax.rsqrt(jnp.mean(v * v, axis=-1, keepdims=True) + EPS)
        r1c[rows, :] = jnp.broadcast_to(scale, (32, 128))
        return 0

    lax.fori_loop(0, 8, scales, 0)
    ids = seg[...].astype(F32)

    def below(v):
        return jnp.sum(jnp.where(ids < v, 1.0, 0.0), axis=(0, 1), keepdims=True)

    own_ids = jnp.concatenate([seg[pl.ds(2 * s, 1), :], seg[pl.ds(2 * s + 1, 1), :]], axis=1).astype(F32)
    first_key = jnp.where(own_ids > 2.5, below(2.5), jnp.where(own_ids > 1.5, below(1.5), jnp.where(own_ids > 0.5, below(0.5), 0.0)))
    first_key = jnp.concatenate([first_key, first_key], axis=1).astype(jnp.int32)
    query_place = s * 256 + lax.broadcasted_iota(jnp.int32, (1, 256), 1)
    query_place = jnp.concatenate([query_place, query_place], axis=1)
    top = jnp.max(ids, axis=(0, 1), keepdims=True)
    kept = below(top)

    ag_kvw.step(1)
    ag_q.step(1)
    load_c.wait()

    def mask_cot(i, _):
        rows = pl.ds(pl.multiple_of(i * 32, 32), 32)
        place = (s * 256 + i * 32 + lax.broadcasted_iota(jnp.int32, (32, 1), 0)).astype(F32)
        g[rows, :] = jnp.where(place < kept, g[rows, :].astype(F32), 0.0).astype(BF16)
        return 0

    lax.fori_loop(0, 8, mask_cot, 0)
    pairs = (s + 2) // 2

    def clear(j, _):
        kvg[j // 4, j % 4] = jnp.zeros((256, 256), BF16)
        return 0

    lax.fori_loop(2 * pairs, 16, clear, 0)
    ag_kvw.step(2)
    ag_q.step(2)
    ag_g.step(1)
    ag_o.step(1)
    ag_d.step(1)
    ag_kvw.step(3)
    ag_q.step(3)
    ag_g.step(2)
    ag_kvw.finish()

    def gain_row(n):
        return jnp.concatenate([wkv[j // 4, j % 4, 128:144, 0:128].astype(F32)[n : n + 1, :] for j in range(16)], axis=1)

    gain1 = gain_row(0)
    gain2 = gain_row(1)

    def norm_in(i, _):
        rows = pl.ds(pl.multiple_of(i * 32, 32), 32)
        v = xb[rows, :].astype(F32) * r1c[rows, 0:1]
        xn[rows, :] = (v * gain1).astype(BF16)
        return 0

    lax.fori_loop(0, 8, norm_in, 0)
    kv[x, z] = nn(xn[...], wkv[:, :, 0:128, :].reshape(2048, 256)).astype(BF16)
    ag_kv.start()
    for d in load_m:
        d.wait()
    ag_mg.start()
    ag_q.finish()
    q = nn(xn[...], wq[...].reshape(2048, 256)).astype(BF16)
    qt[...] = jnp.concatenate([q[:, :128].T, q[:, 128:].T], axis=1)
    ag_kv.step(1)
    ag_o.step(2)
    ag_kv.step(2)
    ag_mg.step(1)
    ag_mu.start()
    for j in range(8):
        xnt[256 * j : 256 * j + 256, :] = xn[:, 256 * j : 256 * j + 256].T
    ag_kv.step(3)
    ag_g.step(3)
    ag_o.step(3)
    ag_mu.step(1)
    ag_d.step(2)
    ag_mg.step(2)
    ag_kv.finish()

    ot[...] = jnp.zeros_like(ot)
    key_line = lax.broadcasted_iota(jnp.int32, (512, 512), 0)

    def scores(i):
        both = kv[i // 2, pl.ds(2 * (i % 2), 2)].reshape(512, 256)
        keys, values = both[:, 0:128], both[:, 128:256]
        place = i * 512 + key_line
        allowed = (place >= first_key) & (place <= query_place)
        return keys, values, jnp.where(allowed, nn(keys, qt[...]) * (SCALE * LOG2E), MASKED)

    def attend(i, state):
        top, total = state
        _, values, st = scores(i)
        new_top = jnp.maximum(top, jnp.max(st, axis=0, keepdims=True))
        probs = jnp.exp2(st - new_top)
        shrink = jnp.exp2(top - new_top)
        ot[...] = ot[...] * shrink + nn(values.T, probs.astype(BF16))
        return new_top, total * shrink + jnp.sum(probs, axis=0, keepdims=True)

    state = (jnp.full((1, 512), FLOOR, F32), jnp.zeros((1, 512), F32))
    top, total = lax.fori_loop(0, pairs, attend, state)
    lse = top + jnp.log(total) * LOG2E
    ot[...] = ot[...] / total
    o = jnp.concatenate([ot[:, 0:256].T, ot[:, 256:512].T], axis=1)
    ob[...] = o
    ag_g.finish()
    gp[...] = nn(xn[...], wg[...].reshape(2048, 256))
    yv = (o * jax.nn.sigmoid(gp[...])).astype(BF16)
    ag_o.finish()
    red = ReduceY(net, part_a, *yb[0])
    for j in range(8):
        w2 = jnp.concatenate([wo[j // 2, 2 * (j % 2) + i] for i in (0, 1)], axis=1)
        part_a[:, :, :, 256 * j : 256 * j + 256] = nn(yv, w2).astype(BF16).reshape(4, 2, 32, 256)
        if j % 4 == 3:
            red.start(j // 4)
    ag_d.step(3)
    red.step(0)
    red.step(1)
    ag_mg.step(3)
    ag_mu.step(2)
    yt = yv.T
    own_rows = pl.ds(pl.multiple_of(net.k * ROWS, ROWS), ROWS)
    h = xb[own_rows, :].astype(F32) + red.finish()
    h32[...] = h
    scale2 = lax.rsqrt(jnp.mean(h * h, axis=-1, keepdims=True) + EPS)
    z2 = h * scale2
    z32[...] = z2
    r32[...] = jnp.broadcast_to(scale2, (ROWS, 128))
    hnb[y, c] = (z2 * gain2).astype(BF16)
    gat = GatherY(net, hnb)
    gat.start()
    ag_d.finish()

    for n in range(3):
        w2 = jnp.concatenate([wd[j // 4, j % 4, 256 * n : 256 * n + 256, :] for j in range(16)], axis=1)
        dmb[:, 256 * n : 256 * n + 256] = nt(g[...], w2)
    gat.step()
    gat.finish()
    hn = hnb[...].reshape(256, 2048)
    for j in range(8):
        hnt[256 * j : 256 * j + 256, :] = hnb[:, :, :, 256 * j : 256 * j + 256].reshape(256, 256).T
    ag_mu.step(3)
    ag_mg.finish()
    for n in range(3):
        ab[:, 256 * n : 256 * n + 256] = nn(hn, wm[:, :, :, 256 * n : 256 * n + 256].reshape(2048, 256))
    ag_mu.finish()
    for n in range(3):
        cols = slice(256 * n, 256 * n + 256)
        up_cols = slice(768 + 256 * n, 1024 + 256 * n)
        a = ab[:, cols]
        u = nn(hn, wm[:, :, :, up_cols].reshape(2048, 256))
        sig = jax.nn.sigmoid(a)
        silu = a * sig
        mt[cols, :] = (silu * u).astype(BF16).T
        dm = dmb[:, cols]
        dadu[:, cols] = (dm * u * sig * (1.0 + a * (1.0 - sig))).astype(BF16)
        dadu[:, up_cols] = (dm * silu).astype(BF16)
    for a in (ag_kvw, ag_q, ag_g, ag_o, ag_d, ag_mg, ag_mu, red):
        a.drain()
    mm = mt[...].T
    for j in range(8):
        w2 = jnp.concatenate([wd[j // 2, 2 * (j % 2) + i] for i in (0, 1)], axis=1)
        part_b[:, :, :, 256 * j : 256 * j + 256] = nn(mm, w2).astype(BF16).reshape(4, 2, 32, 256)
    for j in range(8):
        pd = nn(mt[...], g[:, 256 * j : 256 * j + 256])
        for i in (0, 1):
            wd[j // 2, 2 * (j % 2) + i] = pd[:, 128 * i : 128 * i + 128].astype(BF16)
    rs_d = Scatter(net, wd, 768, sb[0])
    rs_d.start()
    red3 = ReduceY(net, part_a, *yb[1])
    for j in range(8):
        w2 = wm[j // 2, 2 * (j % 2) : 2 * (j % 2) + 2].reshape(256, 1536)
        part_a[:, :, :, 256 * j : 256 * j + 256] = nt(dadu[...], w2).astype(BF16).reshape(4, 2, 32, 256)
        if j % 4 == 3:
            red3.start(j // 4)
    rs_mg = Scatter(net, wm, 128, sb[1], pl.ds(0, 768))
    rs_mu = Scatter(net, wm, 128, sb[2], pl.ds(768, 768))
    red3.step(0)
    for n, rs in ((0, rs_mg), (1, rs_mu)):
        for j in range(8):
            pm = nn(hnt[256 * j : 256 * j + 256, :], dadu[:, 768 * n : 768 * n + 768])
            wm[j // 2, 2 * (j % 2) : 2 * (j % 2) + 2, :, 768 * n : 768 * n + 768] = pm.astype(BF16).reshape(2, 128, 768)
            if n == 0 and j == 3:
                red3.step(1)
        rs.start()
    dhn = red3.finish()
    z2 = z32[...]
    e2 = dhn * gain2
    grads_gain2 = jnp.sum(dhn * z2, axis=0, keepdims=True)
    dh = g[own_rows, :].astype(F32) + r32[:, 0:1] * (e2 - z2 * jnp.mean(e2 * z2, axis=-1, keepdims=True))
    dh32[...] = dh
    dcb[y, c] = dh.astype(BF16)
    gat3 = GatherY(net, dcb)
    gat3.start()
    red2 = ReduceY(net, part_b, *yb[2])
    red2.start(0)
    red2.start(1)
    rs_d.step2()
    gat3.step()
    red2.step(0)
    red2.step(1)
    gat3.finish()
    dc = dcb[...].reshape(256, 2048)
    w2 = jnp.concatenate([wo[j // 4, j % 4] for j in range(16)], axis=1)
    dy = nt(dc, w2)
    sig = jax.nn.sigmoid(gp[...])
    do = (dy * sig).astype(BF16)
    dg = (dy * ob[...] * sig * (1.0 - sig)).astype(BF16)
    dot_[...] = jnp.concatenate([do[:, :128].T, do[:, 128:].T], axis=1)
    q_rows = jnp.concatenate([qt[:, 0:256].T, qt[:, 256:512].T], axis=0)
    do_rows = jnp.concatenate([do[:, :128], do[:, 128:]], axis=0)
    w = jnp.sum(dot_[...].astype(F32) * ot[...], axis=0, keepdims=True)
    dqt[...] = jnp.zeros_like(dqt)
    rs_mg.step2()

    def attend_back(i, _):
        keys, values, st = scores(i)
        probs = jnp.exp2(st - lse)
        dp = nn(values, dot_[...])
        ds = (probs * (dp - w) * SCALE).astype(BF16)
        dk = nn(ds, q_rows).astype(BF16)
        dv = nn(probs.astype(BF16), do_rows).astype(BF16)
        kvg[i // 2, pl.ds(2 * (i % 2), 2)] = jnp.concatenate([dk, dv], axis=1).reshape(2, 256, 256)
        dqt[...] += nn(keys.T, ds)
        return 0

    lax.fori_loop(0, pairs, attend_back, 0)
    rs_kv = Scatter(net, kvg, 256, sb[3])
    rs_kv.start()
    rs_mu.step2()
    for j in range(8):
        po = nn(yt, dcb[:, :, :, 256 * j : 256 * j + 256].reshape(256, 256))
        for i in (0, 1):
            wo[j // 2, 2 * (j % 2) + i] = po[:, 128 * i : 128 * i + 128].astype(BF16)
    rs_o = Scatter(net, wo, 256, sb[4])
    rs_o.start()
    rs_kv.step2()
    dq = jnp.concatenate([dqt[:, 0:256].T, dqt[:, 256:512].T], axis=1).astype(BF16)
    for j in range(8):
        pair = (j // 2, slice(2 * (j % 2), 2 * (j % 2) + 2))
        xnt_j = xnt[256 * j : 256 * j + 256, :]
        xn[:, 256 * j : 256 * j + 256] = (nt(dq, wq[pair].reshape(256, 256)) + nt(dg, wg[pair].reshape(256, 256))).astype(BF16)
        wq[pair] = nn(xnt_j, dq).astype(BF16).reshape(2, 128, 256)
        wg[pair] = nn(xnt_j, dg).astype(BF16).reshape(2, 128, 256)
    rs_g = Scatter(net, wg, 128, sb[5])
    rs_g.start()
    bo[y, c] = (h32[...] + red2.finish()).astype(BF16)
    gat2 = GatherY(net, bo)
    gat2.start()
    rs_kv.step3()
    rs_q = Scatter(net, wq, 128, sb[6])
    rs_q.start()
    rs_d.step3()
    rs_mg.step3()
    rs_kv.step4()
    rs_o.step2()
    rs_g.step2()
    for a in (ag_kv, red3):
        a.drain()

    def store_kv(rows, v):
        kv[0, 0, rows, :] = v.astype(BF16)

    rs_kv.finish(store_kv)
    dkdv = kv[0, 0]
    red4 = ReduceY(net, part_a, *yb[3])
    for j in range(8):
        w2 = wkv[j // 2, 2 * (j % 2) : 2 * (j % 2) + 2, 0:128, :].reshape(256, 256)
        px = nt(dkdv, w2) + xn[:, 256 * j : 256 * j + 256].astype(F32)
        part_a[:, :, :, 256 * j : 256 * j + 256] = px.astype(BF16).reshape(4, 2, 32, 256)
        if j % 4 == 3:
            red4.start(j // 4)
    for j in range(8):
        pk = nn(xnt[256 * j : 256 * j + 256, :], dkdv)
        wkv[j // 2, 2 * (j % 2) : 2 * (j % 2) + 2, 0:128, :] = pk.astype(BF16).reshape(2, 128, 256)
    rs_kvw = Scatter(net, wkv, 128, sb[7])
    rs_kvw.start()
    red4.step(0)
    red4.step(1)
    rs_mu.step3()
    rs_q.step2()
    rs_kvw.step2()
    rs_d.step4()
    rs_mg.step4()
    rs_o.step3()
    rs_g.step3()
    dxn = red4.finish()
    scale1 = r1c[own_rows, 0:1]
    z1 = xb[own_rows, :].astype(F32) * scale1
    e1 = dxn * gain1
    grads_gain1 = jnp.sum(dxn * z1, axis=0, keepdims=True)
    input_grad = dh32[...] + scale1 * (e1 - z1 * jnp.mean(e1 * z1, axis=-1, keepdims=True))
    igb[y, c] = input_grad.astype(BF16)
    gat4 = GatherY(net, igb)
    gat4.start()
    line8 = lax.broadcasted_iota(jnp.int32, (8, 128), 0)
    for j in range(16):
        cols = slice(128 * j, 128 * j + 128)
        gx0[j // 4, j % 4] = jnp.where(line8 == 0, grads_gain1[:, cols], jnp.where(line8 == 1, grads_gain2[:, cols], 0.0))
    sx, sz, sy, sc = ([net.sem(), net.sem()] for _ in range(4))
    for d in (1, 2, 3):
        net.send(gx0.at[(x + d) % 4], gxr.at[d - 1], net.at(dx=d), *sx)
    rs_kvw.step3()
    rs_q.step3()
    rs_mu.step4()
    rs_o.step4()
    rs_g.step4()

    def keep(ref):
        def store(rows, v):
            ref[rows, :] = v

        return store

    net.wait_came(gxr, sx[1])
    gx1[...] = gx0[x] + gxr[0] + gxr[1] + gxr[2]
    for d in (1, 2, 3):
        net.send(gx1.at[(z + d) % 4], gzr.at[d - 1], net.at(dz=d), *sz)
    rs_d.finish(keep(md_f))
    move(md_f, md_out)
    rs_mg.finish(keep(mg_f))
    move(mg_f, mg_out)
    gat2.step()
    rs_kvw.step4()
    rs_q.step4()
    net.wait_came(gzr, sz[1])
    gy[y] = gx1[z] + gzr[0] + gzr[1] + gzr[2]
    for d in (1, 2, 3):
        net.send(gy.at[y], gy.at[y], net.at(dy=d), *sy)
    rs_mu.finish(keep(mu_f))
    move(mu_f, mu_out)
    rs_o.finish(keep(og_f))
    move(og_f, og_out)
    rs_g.finish(keep(gg_f))
    move(gg_f, gg_out)
    gat4.step()

    def store_kvw(rows, v):
        kg_f[rows, :] = v[:, :128]
        vg_f[rows, :] = v[:, 128:]

    gat2.finish()
    move(bo, bo_out)
    net.wait_came(gy.at[0:3], sy[1])
    gc[c] = gy[0] + gy[1] + gy[2] + gy[3]
    net.send(gc.at[c], gc.at[c], net.at(dc=1), *sc)
    rs_q.finish(keep(qg_f))
    move(qg_f, qg_out)
    rs_kvw.finish(store_kvw)
    move(kg_f, kg_out)
    move(vg_f, vg_out)
    gat4.finish()
    move(igb, ig_out)
    net.wait_came(gc.at[0], sc[1])
    gn_f[...] = gc[0] + gc[1]
    move(gn_f.at[pl.ds(0, 1)], gain1_out)
    move(gn_f.at[pl.ds(1, 1)], gain2_out)
    for a in (rs_mg, rs_mu, rs_d, rs_kv, rs_g, rs_q, rs_o, rs_kvw, red2, red4, gat, gat2, gat3, gat4):
        a.drain()
    net.wait_sent(gxr, sx[0])
    net.wait_sent(gzr, sz[0])
    net.wait_sent(gy.at[0:3], sy[0])
    net.wait_sent(gc.at[0], sc[0])
    for d in moved[10:]:
        d.wait()


def place_outputs(*refs):
    ins, outs, bufs, (wide, sems) = refs[:12], refs[12:24], refs[24:36], refs[36:]
    spans = [pl.ds(64 * i, 64) for i in range(4)]
    loads = [pltpu.make_async_copy(ins[1].at[r], bufs[1].at[r], sems.at[i]) for i, r in enumerate(spans)]
    order = [0, 9, 10, 11, 3, 4, 5, 6, 7, 2, 8]
    rest = [pltpu.make_async_copy(ins[i], bufs[i], sems.at[4 + i]) for i in order]
    for d in loads + rest:
        d.start()
    copies = []

    def out(src, dst, n):
        d = pltpu.make_async_copy(src, dst, sems.at[n])
        d.start()
        copies.append(d)

    for i, r in enumerate(spans):
        loads[i].wait()
        wide[r, :] = bufs[1][r, :].astype(F32)
        out(wide.at[r], outs[1].at[r], 16 + i)
    for i, d in zip(order, rest):
        d.wait()
        out(bufs[i], outs[i], 20 + i)
    for d in copies:
        d.wait()


def per_device(inputs, cotangent, segment_ids, attn_gain, query_weight, gate_weight, key_weight, value_weight, output_weight, mlp_gain, mlp_gate, mlp_up, mlp_down):
    v = pltpu.VMEM
    y_rows = (4, 2, ROWS, 2048)
    scratch = [
        v((4, 4, 128, 256), BF16),
        v((4, 4, 128, 256), BF16),
        v((4, 4, 144, 256), BF16),
        v((4, 4, 256, 128), BF16),
        v((4, 4, 128, 1536), BF16),
        v((4, 4, 768, 128), BF16),
        v((4, 4, 256, 256), BF16),
        v((4, 4, 256, 256), BF16),
        v((256, 2048), BF16),
        v((256, 2048), BF16),
        v((2048, 256), BF16),
        v((256, 2048), BF16),
        v(y_rows, BF16),
        v((2048, 256), BF16),
        v(y_rows, BF16),
        v(y_rows, BF16),
        v(y_rows, BF16),
        v(y_rows, BF16),
        v(y_rows, BF16),
    ]
    for _ in range(4):
        scratch += [v((4, ROWS, 2048), BF16), v((3, ROWS, 2048), BF16)]
    scratch += [
        v((256, 128), F32),
        v((256, 256), F32),
        v((256, 256), F32),
        v((128, 512), F32),
        v((128, 512), BF16),
        v((128, 512), BF16),
        v((128, 512), F32),
        v((256, 768), F32),
        v((256, 768), F32),
        v((256, 1536), BF16),
        v((768, 256), BF16),
        v((ROWS, 2048), F32),
        v((ROWS, 2048), F32),
        v((ROWS, 128), F32),
        v((ROWS, 2048), F32),
        v((4, 4, 8, 128), F32),
        v((3, 4, 8, 128), F32),
        v((4, 8, 128), F32),
        v((3, 8, 128), F32),
        v((4, 8, 128), F32),
        v((2, 8, 128), F32),
    ]
    grad_shapes = ((128, 768), (128, 768), (768, 128), (256, 128), (128, 256), (128, 256), (128, 128), (128, 128), (8, 128))
    scratch += [v(dims, F32) for dims in grad_shapes]
    for rows, cols in ((768, 128), (128, 768), (128, 768), (256, 256), (256, 128), (128, 256), (128, 256), (128, 256)):
        scratch += scatter_bufs(rows, cols)
    scratch += [pltpu.SemaphoreType.DMA((324,)), pltpu.SemaphoreType.DMA((24,))]
    whole = pl.BlockSpec(memory_space=pltpu.VMEM)
    there = pl.BlockSpec(memory_space=pl.ANY)
    shape = jax.ShapeDtypeStruct
    out_shape = (
        shape((256, 2048), BF16),
        shape((256, 2048), F32),
        shape((1, 128), F32),
        shape((128, 256), F32),
        shape((128, 256), F32),
        shape((128, 128), F32),
        shape((128, 128), F32),
        shape((256, 128), F32),
        shape((1, 128), F32),
        shape((128, 768), F32),
        shape((128, 768), F32),
        shape((768, 128), F32),
    )
    outs = pl.pallas_call(
        kernel,
        out_shape=(shape(y_rows, BF16), shape(y_rows, BF16)) + out_shape[2:],
        in_specs=[there, there, whole, whole, whole] + [there] * 8,
        out_specs=[there] * 12,
        scratch_shapes=scratch,
        compiler_params=pltpu.CompilerParams(collective_id=0, has_side_effects=True, vmem_limit_bytes=63 << 20),
    )(
        inputs,
        cotangent,
        segment_ids.reshape(32, 128),
        attn_gain.reshape(1, 128),
        mlp_gain.reshape(1, 128),
        query_weight,
        gate_weight,
        key_weight,
        value_weight,
        output_weight,
        mlp_gate,
        mlp_up,
        mlp_down,
    )
    outs = pl.pallas_call(
        place_outputs,
        out_shape=out_shape,
        in_specs=[there] * 12,
        out_specs=[there] * 12,
        scratch_shapes=[v(o.shape, BF16 if i == 1 else o.dtype) for i, o in enumerate(out_shape)] + [v((256, 2048), F32), pltpu.SemaphoreType.DMA((32,))],
        compiler_params=pltpu.CompilerParams(vmem_limit_bytes=60 << 20),
    )(outs[0].reshape(256, 2048), outs[1].reshape(256, 2048), *outs[2:])
    outs = list(outs)
    outs[2] = outs[2].reshape(128)
    outs[8] = outs[8].reshape(128)
    return tuple(outs)


def solution(mesh):
    weights = (P("seq"), P("seq", "kv"), P("seq", "kv"), P("seq", "kv"), P("seq", "kv"), P("kv", "seq"))
    weights += (P("seq"), P("seq", "kv"), P("seq", "kv"), P("kv", "seq"))
    return jax.shard_map(
        per_device,
        mesh=mesh,
        in_specs=(P("seq", None), P("seq", None), P()) + weights,
        out_specs=(P("seq", None), P("seq", None)) + weights,
        check_vma=False,
    )
```

time: 217 us -> 191 us (0.88)
  Pallas kernels: 202 us -> 190 us
  local copies, waits for them, and re-layouts: 11.6 us -> 0 us
    pallas_call x1 -> x2, Pallas kernels: 202 us -> 190 us  [the longest x1 186 us: per_device(): pl.pallas_call(kernel, out_shape=(shape(y_rows, BF16), shape(y_rows, BF16...]
    unnamed x34 -> x0, local copies, waits for them, and re-layouts: 10.3 us -> none
where the time goes in v2:
time: 191 us
  Pallas kernels  190 us (99%)
    pallas_call x1, Pallas kernels, per_device(): pl.pallas_call(kernel, out_shape=(shape(y_rows, BF16), shape(y_rows, BF16...  186 us

profile of v2, /device:TPU:1, one launch (start us, length us, event | category | flops | bytes accessed | tf_op | source)
XLA Modules:
  0.0 190.8 jit_solution(7829890761940740454)
XLA Ops:
  0.6 186.5 %shard_map.220 = (bf16[4,2,32,2048]{3,2,1,0:T(8,128)(2,1)}, bf16[4,2,32,2048]{3,2,1,0:T(8,128)(2,1)}, f32[1,128]{1,0:T(1,128)}, f32[128,256]{1,0:T(8,128)}, f32[...) custom-call(bf16[256,2048]{1,0:T(8,128)(2,1)} %refs_0_.1, ...), custom_call_target="tpu_custom_call" | custom-call | tf_op jit(solution)/shard_map/pallas_call | solution.py:848
  187.1 3.5 %shard_map.221 = (bf16[256,2048]{1,0:T(8,128)(2,1)}, f32[256,2048]{1,0:T(8,128)}, f32[1,128]{1,0:T(1,128)}, f32[128,256]{1,0:T(8,128)}, f32[128,256]{1,0:T(8,128...) custom-call(bf16[256,2048]{1,0:T(8,128)(2,1)} %bitcast.7, ...), custom_call_target="tpu_custom_call" | custom-call | tf_op jit(solution)/shard_map/pallas_call | solution.py:870

commit v3 on v2

--- a/solution.py
+++ b/solution.py
@@ -27,6 +27,10 @@
     return lax.dot_general(left, right, (((1,), (1,)), ((), ())), preferred_element_type=F32)
 
 
+def half_rows(n):
+    return pl.ds(16 * n, 16)
+
+
 class Net:
     def __init__(self, sems):
         s, k = lax.axis_index("seq"), lax.axis_index("kv")
@@ -80,9 +84,11 @@
         self.net, self.w, self.cols = net, w, cols
         q, h, q2, r = cuts
         self.spans = ((0, q, h), (h, q2, r))
-        self.rows = pl.ds(0, r)
-        self.sent = [net.sem() for _ in range(4)]
-        self.came = [[[net.sem(), net.sem()], [net.sem()], [net.sem(), net.sem()], [net.sem()]] for _ in (0, 1)]
+        self.sent = [net.sem() for _ in range(2)]
+        self.came = [net.sem() for _ in range(4)]
+        rows = pl.ds(0, r)
+        self.sizes = [w.at[0, 0:2, rows, cols], w.at[0, 0, rows, cols], w.at[0:2, :, rows, cols], w.at[0, :, rows, cols]]
+        self.totals = [w.at[0, 0:3, rows, cols], w.at[0:3, :, rows, cols]]
 
     def part(self, o, n):
         r0, r1, r2 = self.spans[o]
@@ -96,55 +102,47 @@
         rows = self.part(o, n)
         return self.w.at[:, b, rows, self.cols] if o == 0 else self.w.at[b, :, rows, self.cols]
 
-    def push(self, o, n, ref, axis, d, sem):
-        self.net.send(ref, ref, self.net.along(axis, d), self.sent[n], sem)
+    def push(self, n, ref, axis, d):
+        self.net.send(ref, ref, self.net.along(axis, d), self.sent[n // 2], self.came[n])
 
     def start(self):
         for o in (0, 1):
             own = self.single(o, (self.net.x, self.net.z)[o], 0)
-            self.push(o, 0, own, o, 1, self.came[o][0][0])
-            self.push(o, 0, own, o, -1, self.came[o][0][1])
+            self.push(0, own, o, 1)
+            self.push(0, own, o, -1)
 
     def step(self, n):
         net = self.net
+        net.wait_came(self.sizes[n - 1], self.came[n - 1])
         for o in (0, 1):
             me, other = (net.x, net.z) if o == 0 else (net.z, net.x)
-            came = self.came[o]
             if n == 1:
-                low, high = (me + 3) % 4, (me + 1) % 4
-                net.wait_came(self.single(o, low, 0), came[0][0])
-                self.push(o, 1, self.single(o, low, 1), o, 1, came[1][0])
-                net.wait_came(self.single(o, high, 0), came[0][1])
-                self.push(o, 1, self.single(o, high, 2), o, -1, came[1][0])
+                self.push(1, self.single(o, (me + 3) % 4, 1), o, 1)
+                self.push(1, self.single(o, (me + 1) % 4, 2), o, -1)
             elif n == 2:
-                net.wait_came(self.single(o, (me + 2) % 4, 0), came[1][0])
                 own = self.bundle(o, other, 0)
-                self.push(o, 2, own, 1 - o, 1, came[2][0])
-                self.push(o, 2, own, 1 - o, -1, came[2][1])
+                self.push(2, own, 1 - o, 1)
+                self.push(2, own, 1 - o, -1)
             else:
-                low, high = (other + 3) % 4, (other + 1) % 4
-                net.wait_came(self.bundle(o, low, 0), came[2][0])
-                self.push(o, 3, self.bundle(o, low, 1), 1 - o, 1, came[3][0])
-                net.wait_came(self.bundle(o, high, 0), came[2][1])
-                self.push(o, 3, self.bundle(o, high, 2), 1 - o, -1, came[3][0])
+                self.push(3, self.bundle(o, (other + 3) % 4, 1), 1 - o, 1)
+                self.push(3, self.bundle(o, (other + 1) % 4, 2), 1 - o, -1)
 
     def finish(self):
-        for o in (0, 1):
-            other = self.net.z if o == 0 else self.net.x
-            self.net.wait_came(self.bundle(o, (other + 2) % 4, 0), self.came[o][3][0])
+        self.net.wait_came(self.sizes[3], self.came[3])
 
     def drain(self):
-        w, rows, cols = self.w, self.rows, self.cols
-        for ref, sem in zip((w.at[0, 0:2, rows, cols], w.at[0, 0, rows, cols], w.at[0:2, :, rows, cols], w.at[0, :, rows, cols]), self.sent):
+        for ref, sem in zip(self.totals, self.sent):
             self.net.wait_sent(ref, sem)
 
 
 class Scatter:
     def __init__(self, net, p, rows, bufs, cols=slice(None)):
         self.net, self.p, self.bufs, self.cols = net, p, bufs, cols
-        self.r, self.h, self.q = rows, rows // 2, rows // 4
+        self.h, self.q = rows // 2, rows // 4
         self.sent = [net.sem(), net.sem()]
-        self.came = [[[net.sem(), net.sem()] for _ in range(4)] for _ in (0, 1)]
+        self.came = [net.sem() for _ in range(4)]
+        whole = pl.ds(0, rows)
+        self.totals = [p.at[0:3, :, whole, cols], p.at[0, 0:3, whole, cols]]
 
     def rows(self, o, part):
         base = o * self.h
@@ -168,24 +166,27 @@
     def half(self, side):
         return pl.ds(side * self.q, self.q)
 
+    def push(self, n, src, dst, axis, d):
+        self.net.send(src, dst, self.net.along(axis, d), self.sent[n // 2], self.came[n])
+
     def start(self):
         r1, r2 = self.bufs[0], self.bufs[1]
         for o in (0, 1):
             me, _ = self.place(o)
             for side, d in ((0, 1), (1, -1)):
-                self.net.send(self.bundle(o, (me + 2) % 4, 1 + side), r1.at[o, side], self.net.along(o, d), self.sent[0], self.came[o][0][side])
+                self.push(0, self.bundle(o, (me + 2) % 4, 1 + side), r1.at[o, side], o, d)
         for o in (0, 1):
             me, _ = self.place(o)
             for side, d in ((0, 1), (1, -1)):
-                self.net.send(self.bundle(o, (me + d) % 4, 2 - side), r2.at[o, side, :, self.half(1 - side)], self.net.along(o, d), self.sent[0], self.came[o][1][side])
+                self.push(1, self.bundle(o, (me + d) % 4, 2 - side), r2.at[o, side, :, self.half(1 - side)], o, d)
 
     def step2(self):
         r1, r2 = self.bufs[0], self.bufs[1]
+        self.net.wait_came(r1, self.came[0])
         for o in (0, 1):
             me, _ = self.place(o)
             for side, d in ((0, 1), (1, -1)):
                 a, part = (me + d) % 4, 1 + side
-                self.net.wait_came(r1.at[o, side], self.came[o][0][side])
 
                 def add(i, _, o=o, a=a, part=part, side=side):
                     b = self.block(o, a, i, part)
@@ -193,14 +194,13 @@
                     return 0
 
                 lax.fori_loop(0, 4, add, 0)
-                self.net.send(self.bundle(o, a, part), r2.at[o, side, :, self.half(side)], self.net.along(o, d), self.sent[0], self.came[o][1][side])
+                self.push(1, self.bundle(o, a, part), r2.at[o, side, :, self.half(side)], o, d)
 
     def step3(self):
         r2, r3, r4 = self.bufs[1], self.bufs[2], self.bufs[3]
+        self.net.wait_came(r2, self.came[1])
         for o in (0, 1):
             me, other = self.place(o)
-            for side in (0, 1):
-                self.net.wait_came(r2.at[o, side], self.came[o][1][side])
 
             def add(i, o=o, me=me):
                 b = self.block(o, me, i, 0)
@@ -213,34 +213,32 @@
 
             add((other + 2) % 4)
             for side, d in ((0, 1), (1, -1)):
-                self.net.send(self.block(o, me, (other + 2) % 4, 1 + side), r3.at[o, side], self.net.along(1 - o, d), self.sent[1], self.came[o][2][side])
+                self.push(2, self.block(o, me, (other + 2) % 4, 1 + side), r3.at[o, side], 1 - o, d)
             lax.fori_loop(1, 4, far, 0)
             for side, d in ((0, 1), (1, -1)):
-                self.net.send(self.block(o, me, (other + d) % 4, 2 - side), r4.at[o, side, self.half(1 - side)], self.net.along(1 - o, d), self.sent[1], self.came[o][3][side])
+                self.push(3, self.block(o, me, (other + d) % 4, 2 - side), r4.at[o, side, self.half(1 - side)], 1 - o, d)
 
     def step4(self):
         r3, r4 = self.bufs[2], self.bufs[3]
+        self.net.wait_came(r3, self.came[2])
         for o in (0, 1):
             me, other = self.place(o)
             for side, d in ((0, 1), (1, -1)):
-                self.net.wait_came(r3.at[o, side], self.came[o][2][side])
                 b = self.block(o, me, (other + d) % 4, 1 + side)
                 b[...] = (b[...].astype(F32) + r3[o, side].astype(F32)).astype(BF16)
-                self.net.send(b, r4.at[o, side, self.half(side)], self.net.along(1 - o, d), self.sent[1], self.came[o][3][side])
+                self.push(3, b, r4.at[o, side, self.half(side)], 1 - o, d)
 
     def finish(self, store):
         r4 = self.bufs[3]
+        self.net.wait_came(r4, self.came[3])
         for o in (0, 1):
             me, other = self.place(o)
-            for side in (0, 1):
-                self.net.wait_came(r4.at[o, side], self.came[o][3][side])
             total = self.block(o, me, other, 0)[...].astype(F32) + r4[o, 0].astype(F32) + r4[o, 1].astype(F32)
             store(self.rows(o, 0), total)
 
     def drain(self):
-        rows = pl.ds(0, self.r)
-        self.net.wait_sent(self.p.at[0:3, :, rows, self.cols], self.sent[0])
-        self.net.wait_sent(self.p.at[0, 0:3, rows, self.cols], self.sent[1])
+        for ref, sem in zip(self.totals, self.sent):
+            self.net.wait_sent(ref, sem)
 
 
 def scatter_bufs(rows, cols):
@@ -256,29 +254,26 @@
 class ReduceY:
     def __init__(self, net, part, cr, yr):
         self.net, self.part, self.cr, self.yr = net, part, cr, yr
-        self.sent, self.came, self.core = [net.sem(), net.sem()], net.sem(), [net.sem(), net.sem()]
-
-    def cols(self, n):
-        return pl.ds(1024 * n, 1024)
+        self.sent, self.core, self.far = [net.sem(), net.sem()], [net.sem(), net.sem()], [net.sem(), net.sem()]
 
     def start(self, n):
-        net, cols = self.net, self.cols(n)
-        net.send(self.part.at[:, 1 - net.c, :, cols], self.cr.at[:, :, cols], net.at(dc=1), self.sent[0], self.core[n])
+        net, rows = self.net, half_rows(n)
+        net.send(self.part.at[:, 1 - net.c, rows], self.cr.at[:, rows], net.at(dc=1), self.sent[0], self.core[n])
 
     def step(self, n):
-        net, cols = self.net, self.cols(n)
-        net.wait_came(self.cr.at[:, :, cols], self.core[n])
+        net, rows = self.net, half_rows(n)
+        net.wait_came(self.cr.at[:, rows], self.core[n])
         for d in (2, 1, 3):
             to = (net.y + d) % 4
-            own = self.part.at[to, net.c, :, cols]
-            own[...] = (own[...].astype(F32) + self.cr[to, :, cols].astype(F32)).astype(BF16)
-            net.send(own, self.yr.at[d - 1, :, cols], net.at(dy=d), self.sent[1], self.came)
-
-    def finish(self):
-        net = self.net
-        total = self.part[net.y, net.c].astype(F32) + self.cr[net.y].astype(F32)
-        net.wait_came(self.yr, self.came)
-        return total + self.yr[0].astype(F32) + self.yr[1].astype(F32) + self.yr[2].astype(F32)
+            own = self.part.at[to, net.c, rows]
+            own[...] = (own[...].astype(F32) + self.cr[to, rows].astype(F32)).astype(BF16)
+            net.send(own, self.yr.at[d - 1, rows], net.at(dy=d), self.sent[1], self.far[n])
+
+    def finish(self, n):
+        net, rows, yr = self.net, half_rows(n), self.yr
+        total = self.part[net.y, net.c, rows].astype(F32) + self.cr[net.y, rows].astype(F32)
+        net.wait_came(yr.at[:, rows], self.far[n])
+        return total + yr[0, rows].astype(F32) + yr[1, rows].astype(F32) + yr[2, rows].astype(F32)
 
     def drain(self):
         self.net.wait_sent(self.cr, self.sent[0])
@@ -288,21 +283,22 @@
 class GatherY:
     def __init__(self, net, g):
         self.net, self.g = net, g
-        self.sent, self.near, self.far = [net.sem(), net.sem()], net.sem(), [net.sem() for _ in range(3)]
-
-    def start(self):
-        n = self.net
-        own = self.g.at[n.y, n.c]
-        for d in (1, 2, 3):
-            n.send(own, own, n.at(dy=d), self.sent[0], self.far[d - 1])
-        n.send(own, own, n.at(dc=1), self.sent[1], self.near)
-
-    def step(self):
-        n = self.net
+        self.sent, self.near, self.far = [net.sem(), net.sem()], net.sem(), [[net.sem() for _ in range(3)] for _ in range(2)]
+
+    def put(self, n, rows):
+        net = self.net
+        own = self.g.at[net.y, net.c, half_rows(n)]
+        own[...] = rows.astype(BF16)
+        for d in (2, 1, 3):
+            net.send(own, own, net.at(dy=d), self.sent[0], self.far[n][d - 1])
+        net.send(own, own, net.at(dc=1), self.sent[1], self.near)
+
+    def step(self, n):
+        net = self.net
         for d in (1, 3, 2):
-            came = self.g.at[(n.y + 4 - d) % 4, n.c]
-            n.wait_came(came, self.far[d - 1])
-            n.send(came, came, n.at(dc=1), self.sent[1], self.near)
+            came = self.g.at[(net.y + 4 - d) % 4, net.c, half_rows(n)]
+            net.wait_came(came, self.far[n][d - 1])
+            net.send(came, came, net.at(dc=1), self.sent[1], self.near)
 
     def finish(self):
         self.net.wait_came(self.g.at[:, 1 - self.net.c], self.near)
@@ -320,7 +316,7 @@
 
     x_in, cot_in, seg, gain_a, gain_b, wq_in, wg_in, wk_in, wv_in, wo_in, mg_in, mu_in, md_in = take(13)
     bo_out, ig_out, gain1_out, qg_out, gg_out, kg_out, vg_out, og_out, gain2_out, mg_out, mu_out, md_out = take(12)
-    wq, wg, wkv, wo, wm, wd, kv, kvg = take(8)
+    wq, wg, wkv, wo, wm, wd, kv, kvg, pd0, pd1 = take(10)
     xb, xn, xnt, g, hnb, hnt, dcb, igb, bo = take(9)
     part_a, part_b = take(2)
     yb = [take(2) for _ in range(4)]
@@ -328,7 +324,7 @@
     h32, z32, r32, dh32 = take(4)
     gx0, gxr, gx1, gzr, gy, gc = take(6)
     mg_f, mu_f, md_f, og_f, qg_f, gg_f, kg_f, vg_f, gn_f = take(9)
-    sb = [take(4) for _ in range(8)]
+    sb = [take(4) for _ in range(10)]
     sems, local = take(2)
 
     net = Net(sems)
@@ -361,7 +357,7 @@
     ag_kv = Gather(net, kv, (64, 128, 192, 256))
     ag_d = Gather(net, wd, (192, 384, 576, 768))
     ag_mg = Gather(net, wm, (32, 64, 96, 128), pl.ds(0, 768))
-    ag_mu = Gather(net, wm, (32, 64, 96, 128), pl.ds(768, 768))
+    ag_mu = [Gather(net, wm, (32, 64, 96, 128), pl.ds(768 + 384 * n, 384)) for n in (0, 1)]
     for d in load_kv:
         d.wait()
     ag_kvw.start()
@@ -450,13 +446,15 @@
     ag_o.step(2)
     ag_kv.step(2)
     ag_mg.step(1)
-    ag_mu.start()
+    for a in ag_mu:
+        a.start()
     for j in range(8):
         xnt[256 * j : 256 * j + 256, :] = xn[:, 256 * j : 256 * j + 256].T
     ag_kv.step(3)
     ag_g.step(3)
     ag_o.step(3)
-    ag_mu.step(1)
+    for a in ag_mu:
+        a.step(1)
     ag_d.step(2)
     ag_mg.step(2)
     ag_kv.finish()
@@ -494,94 +492,107 @@
     for j in range(8):
         w2 = jnp.concatenate([wo[j // 2, 2 * (j % 2) + i] for i in (0, 1)], axis=1)
         part_a[:, :, :, 256 * j : 256 * j + 256] = nn(yv, w2).astype(BF16).reshape(4, 2, 32, 256)
-        if j % 4 == 3:
-            red.start(j // 4)
+    for n in (0, 1):
+        red.start(n)
     ag_d.step(3)
-    red.step(0)
-    red.step(1)
+    for n in (0, 1):
+        red.step(n)
     ag_mg.step(3)
-    ag_mu.step(2)
+    for a in ag_mu:
+        a.step(2)
     yt = yv.T
-    own_rows = pl.ds(pl.multiple_of(net.k * ROWS, ROWS), ROWS)
-    h = xb[own_rows, :].astype(F32) + red.finish()
-    h32[...] = h
-    scale2 = lax.rsqrt(jnp.mean(h * h, axis=-1, keepdims=True) + EPS)
-    z2 = h * scale2
-    z32[...] = z2
-    r32[...] = jnp.broadcast_to(scale2, (ROWS, 128))
-    hnb[y, c] = (z2 * gain2).astype(BF16)
+    own_rows = [pl.ds(pl.multiple_of(net.k * ROWS + 16 * n, 16), 16) for n in (0, 1)]
     gat = GatherY(net, hnb)
-    gat.start()
+    for n in (0, 1):
+        h = xb[own_rows[n], :].astype(F32) + red.finish(n)
+        h32[half_rows(n), :] = h
+        scale2 = lax.rsqrt(jnp.mean(h * h, axis=-1, keepdims=True) + EPS)
+        z2 = h * scale2
+        z32[half_rows(n), :] = z2
+        r32[half_rows(n), :] = jnp.broadcast_to(scale2, (16, 128))
+        gat.put(n, z2 * gain2)
     ag_d.finish()
 
     for n in range(3):
         w2 = jnp.concatenate([wd[j // 4, j % 4, 256 * n : 256 * n + 256, :] for j in range(16)], axis=1)
         dmb[:, 256 * n : 256 * n + 256] = nt(g[...], w2)
-    gat.step()
+    for n in (0, 1):
+        gat.step(n)
     gat.finish()
     hn = hnb[...].reshape(256, 2048)
     for j in range(8):
         hnt[256 * j : 256 * j + 256, :] = hnb[:, :, :, 256 * j : 256 * j + 256].reshape(256, 256).T
-    ag_mu.step(3)
+    ag_mu[0].step(3)
     ag_mg.finish()
     for n in range(3):
         ab[:, 256 * n : 256 * n + 256] = nn(hn, wm[:, :, :, 256 * n : 256 * n + 256].reshape(2048, 256))
-    ag_mu.finish()
-    for n in range(3):
-        cols = slice(256 * n, 256 * n + 256)
-        up_cols = slice(768 + 256 * n, 1024 + 256 * n)
+    ag_mu[1].step(3)
+    for a in (ag_kvw, ag_q, ag_g, ag_o, red):
+        a.drain()
+    pds = (pd0, pd1)
+    rs_d = [Scatter(net, pds[n], 384, sb[n]) for n in (0, 1)]
+
+    def down_grad(n):
+        for j in range(8):
+            pd = nn(mt[384 * n : 384 * n + 384, :], g[:, 256 * j : 256 * j + 256])
+            for i in (0, 1):
+                pds[n][j // 2, 2 * (j % 2) + i] = pd[:, 128 * i : 128 * i + 128].astype(BF16)
+        rs_d[n].start()
+
+    for n in (0, 1):
+        cols = slice(384 * n, 384 * n + 384)
+        up_cols = slice(768 + 384 * n, 1152 + 384 * n)
+        ag_mu[n].finish()
         a = ab[:, cols]
-        u = nn(hn, wm[:, :, :, up_cols].reshape(2048, 256))
+        u = nn(hn, wm[:, :, :, up_cols].reshape(2048, 384))
         sig = jax.nn.sigmoid(a)
         silu = a * sig
         mt[cols, :] = (silu * u).astype(BF16).T
         dm = dmb[:, cols]
         dadu[:, cols] = (dm * u * sig * (1.0 + a * (1.0 - sig))).astype(BF16)
         dadu[:, up_cols] = (dm * silu).astype(BF16)
-    for a in (ag_kvw, ag_q, ag_g, ag_o, ag_d, ag_mg, ag_mu, red):
+        if n == 0:
+            down_grad(0)
+    red3 = ReduceY(net, part_a, *yb[1])
+    for j in range(8):
+        w2 = wm[j // 2, 2 * (j % 2) : 2 * (j % 2) + 2].reshape(256, 1536)
+        part_a[:, :, :, 256 * j : 256 * j + 256] = nt(dadu[...], w2).astype(BF16).reshape(4, 2, 32, 256)
+    for n in (0, 1):
+        red3.start(n)
+    down_grad(1)
+    for a in (ag_d, ag_mg, *ag_mu):
         a.drain()
+    rs_m = [Scatter(net, wm, 128, sb[2 + n], pl.ds(768 * n, 768)) for n in (0, 1)]
+    for n in (0, 1):
+        for j in range(8):
+            pm = nn(hnt[256 * j : 256 * j + 256, :], dadu[:, 768 * n : 768 * n + 768])
+            wm[j // 2, 2 * (j % 2) : 2 * (j % 2) + 2, :, 768 * n : 768 * n + 768] = pm.astype(BF16).reshape(2, 128, 768)
+        rs_m[n].start()
+        if n == 0:
+            red3.step(0)
+            red3.step(1)
     mm = mt[...].T
     for j in range(8):
         w2 = jnp.concatenate([wd[j // 2, 2 * (j % 2) + i] for i in (0, 1)], axis=1)
         part_b[:, :, :, 256 * j : 256 * j + 256] = nn(mm, w2).astype(BF16).reshape(4, 2, 32, 256)
-    for j in range(8):
-        pd = nn(mt[...], g[:, 256 * j : 256 * j + 256])
-        for i in (0, 1):
-            wd[j // 2, 2 * (j % 2) + i] = pd[:, 128 * i : 128 * i + 128].astype(BF16)
-    rs_d = Scatter(net, wd, 768, sb[0])
-    rs_d.start()
-    red3 = ReduceY(net, part_a, *yb[1])
-    for j in range(8):
-        w2 = wm[j // 2, 2 * (j % 2) : 2 * (j % 2) + 2].reshape(256, 1536)
-        part_a[:, :, :, 256 * j : 256 * j + 256] = nt(dadu[...], w2).astype(BF16).reshape(4, 2, 32, 256)
-        if j % 4 == 3:
-            red3.start(j // 4)
-    rs_mg = Scatter(net, wm, 128, sb[1], pl.ds(0, 768))
-    rs_mu = Scatter(net, wm, 128, sb[2], pl.ds(768, 768))
-    red3.step(0)
-    for n, rs in ((0, rs_mg), (1, rs_mu)):
-        for j in range(8):
-            pm = nn(hnt[256 * j : 256 * j + 256, :], dadu[:, 768 * n : 768 * n + 768])
-            wm[j // 2, 2 * (j % 2) : 2 * (j % 2) + 2, :, 768 * n : 768 * n + 768] = pm.astype(BF16).reshape(2, 128, 768)
-            if n == 0 and j == 3:
-                red3.step(1)
-        rs.start()
-    dhn = red3.finish()
-    z2 = z32[...]
-    e2 = dhn * gain2
-    grads_gain2 = jnp.sum(dhn * z2, axis=0, keepdims=True)
-    dh = g[own_rows, :].astype(F32) + r32[:, 0:1] * (e2 - z2 * jnp.mean(e2 * z2, axis=-1, keepdims=True))
-    dh32[...] = dh
-    dcb[y, c] = dh.astype(BF16)
+    grads_gain2 = jnp.zeros((1, 2048), F32)
     gat3 = GatherY(net, dcb)
-    gat3.start()
+    for n in (0, 1):
+        dhn = red3.finish(n)
+        z2 = z32[half_rows(n), :]
+        e2 = dhn * gain2
+        grads_gain2 += jnp.sum(dhn * z2, axis=0, keepdims=True)
+        dh = g[own_rows[n], :].astype(F32) + r32[half_rows(n), 0:1] * (e2 - z2 * jnp.mean(e2 * z2, axis=-1, keepdims=True))
+        dh32[half_rows(n), :] = dh
+        gat3.put(n, dh)
     red2 = ReduceY(net, part_b, *yb[2])
-    red2.start(0)
-    red2.start(1)
-    rs_d.step2()
-    gat3.step()
-    red2.step(0)
-    red2.step(1)
+    for n in (0, 1):
+        red2.start(n)
+    rs_d[0].step2()
+    for n in (0, 1):
+        gat3.step(n)
+    for n in (0, 1):
+        red2.step(n)
     gat3.finish()
     dc = dcb[...].reshape(256, 2048)
     w2 = jnp.concatenate([wo[j // 4, j % 4] for j in range(16)], axis=1)
@@ -594,7 +605,7 @@
     do_rows = jnp.concatenate([do[:, :128], do[:, 128:]], axis=0)
     w = jnp.sum(dot_[...].astype(F32) * ot[...], axis=0, keepdims=True)
     dqt[...] = jnp.zeros_like(dqt)
-    rs_mg.step2()
+    rs_d[1].step2()
 
     def attend_back(i, _):
         keys, values, st = scores(i)
@@ -608,16 +619,16 @@
         return 0
 
     lax.fori_loop(0, pairs, attend_back, 0)
-    rs_kv = Scatter(net, kvg, 256, sb[3])
-    rs_kv.start()
-    rs_mu.step2()
+    rs_kv = [Scatter(net, kvg, 256, sb[4 + 5 * n], pl.ds(128 * n, 128)) for n in (0, 1)]
+    for a in rs_kv:
+        a.start()
     for j in range(8):
         po = nn(yt, dcb[:, :, :, 256 * j : 256 * j + 256].reshape(256, 256))
         for i in (0, 1):
             wo[j // 2, 2 * (j % 2) + i] = po[:, 128 * i : 128 * i + 128].astype(BF16)
-    rs_o = Scatter(net, wo, 256, sb[4])
-    rs_o.start()
-    rs_kv.step2()
+    for a in rs_kv:
+        a.step2()
+    rs_m[0].step2()
     dq = jnp.concatenate([dqt[:, 0:256].T, dqt[:, 256:512].T], axis=1).astype(BF16)
     for j in range(8):
         pair = (j // 2, slice(2 * (j % 2), 2 * (j % 2) + 2))
@@ -625,120 +636,134 @@
         xn[:, 256 * j : 256 * j + 256] = (nt(dq, wq[pair].reshape(256, 256)) + nt(dg, wg[pair].reshape(256, 256))).astype(BF16)
         wq[pair] = nn(xnt_j, dq).astype(BF16).reshape(2, 128, 256)
         wg[pair] = nn(xnt_j, dg).astype(BF16).reshape(2, 128, 256)
-    rs_g = Scatter(net, wg, 128, sb[5])
+    rs_g = Scatter(net, wg, 128, sb[6])
     rs_g.start()
-    bo[y, c] = (h32[...] + red2.finish()).astype(BF16)
+    for a in rs_kv:
+        a.step3()
+    rs_o = Scatter(net, wo, 256, sb[5])
+    rs_o.start()
+    rs_d[0].step3()
+    for a in rs_kv:
+        a.step4()
+    rs_q = Scatter(net, wq, 128, sb[7])
+    rs_q.start()
+    rs_m[1].step2()
+    rs_d[1].step3()
     gat2 = GatherY(net, bo)
-    gat2.start()
-    rs_kv.step3()
-    rs_q = Scatter(net, wq, 128, sb[6])
-    rs_q.start()
-    rs_d.step3()
-    rs_mg.step3()
-    rs_kv.step4()
-    rs_o.step2()
-    rs_g.step2()
+    for n in (0, 1):
+        gat2.put(n, h32[half_rows(n), :] + red2.finish(n))
     for a in (ag_kv, red3):
         a.drain()
 
-    def store_kv(rows, v):
-        kv[0, 0, rows, :] = v.astype(BF16)
-
-    rs_kv.finish(store_kv)
+    for n in (0, 1):
+
+        def store_kv(rows, v, n=n):
+            kv[0, 0, rows, 128 * n : 128 * n + 128] = v.astype(BF16)
+
+        rs_kv[n].finish(store_kv)
     dkdv = kv[0, 0]
     red4 = ReduceY(net, part_a, *yb[3])
     for j in range(8):
         w2 = wkv[j // 2, 2 * (j % 2) : 2 * (j % 2) + 2, 0:128, :].reshape(256, 256)
         px = nt(dkdv, w2) + xn[:, 256 * j : 256 * j + 256].astype(F32)
         part_a[:, :, :, 256 * j : 256 * j + 256] = px.astype(BF16).reshape(4, 2, 32, 256)
-        if j % 4 == 3:
-            red4.start(j // 4)
+    for n in (0, 1):
+        red4.start(n)
+    line8 = lax.broadcasted_iota(jnp.int32, (8, 128), 0)
     for j in range(8):
-        pk = nn(xnt[256 * j : 256 * j + 256, :], dkdv)
+        cols = slice(256 * j, 256 * j + 256)
+        pk = nn(xnt[cols, :], dkdv)
         wkv[j // 2, 2 * (j % 2) : 2 * (j % 2) + 2, 0:128, :] = pk.astype(BF16).reshape(2, 128, 256)
-    rs_kvw = Scatter(net, wkv, 128, sb[7])
+        z1 = xb[:, cols].astype(F32) * r1c[:, 0:1]
+        gain1_part = jnp.sum(part_a[:, :, :, cols].reshape(256, 256).astype(F32) * z1, axis=0, keepdims=True)
+        for i in (0, 1):
+            own = slice(128 * i, 128 * i + 128)
+            both = jnp.where(line8 == 1, grads_gain2[:, 256 * j + 128 * i : 256 * j + 128 * i + 128], 0.0)
+            gx0[j // 2, 2 * (j % 2) + i] = jnp.where(line8 == 0, gain1_part[:, own], both)
+    rs_kvw = Scatter(net, wkv, 128, sb[8])
     rs_kvw.start()
-    red4.step(0)
-    red4.step(1)
-    rs_mu.step3()
-    rs_q.step2()
-    rs_kvw.step2()
-    rs_d.step4()
-    rs_mg.step4()
-    rs_o.step3()
-    rs_g.step3()
-    dxn = red4.finish()
-    scale1 = r1c[own_rows, 0:1]
-    z1 = xb[own_rows, :].astype(F32) * scale1
-    e1 = dxn * gain1
-    grads_gain1 = jnp.sum(dxn * z1, axis=0, keepdims=True)
-    input_grad = dh32[...] + scale1 * (e1 - z1 * jnp.mean(e1 * z1, axis=-1, keepdims=True))
-    igb[y, c] = input_grad.astype(BF16)
-    gat4 = GatherY(net, igb)
-    gat4.start()
-    line8 = lax.broadcasted_iota(jnp.int32, (8, 128), 0)
-    for j in range(16):
-        cols = slice(128 * j, 128 * j + 128)
-        gx0[j // 4, j % 4] = jnp.where(line8 == 0, grads_gain1[:, cols], jnp.where(line8 == 1, grads_gain2[:, cols], 0.0))
+    for n in (0, 1):
+        red4.step(n)
     sx, sz, sy, sc = ([net.sem(), net.sem()] for _ in range(4))
     for d in (1, 2, 3):
         net.send(gx0.at[(x + d) % 4], gxr.at[d - 1], net.at(dx=d), *sx)
-    rs_kvw.step3()
-    rs_q.step3()
-    rs_mu.step4()
-    rs_o.step4()
-    rs_g.step4()
-
-    def keep(ref):
-        def store(rows, v):
-            ref[rows, :] = v
-
-        return store
-
+    rs_m[0].step3()
+    rs_o.step2()
+    rs_g.step2()
+    rs_q.step2()
+    rs_kvw.step2()
+    rs_m[1].step3()
+    for a in rs_d:
+        a.step4()
     net.wait_came(gxr, sx[1])
     gx1[...] = gx0[x] + gxr[0] + gxr[1] + gxr[2]
     for d in (1, 2, 3):
         net.send(gx1.at[(z + d) % 4], gzr.at[d - 1], net.at(dz=d), *sz)
-    rs_d.finish(keep(md_f))
+    gat4 = GatherY(net, igb)
+    for n in (0, 1):
+        dxn = red4.finish(n)
+        scale1 = r1c[own_rows[n], 0:1]
+        z1 = xb[own_rows[n], :].astype(F32) * scale1
+        e1 = dxn * gain1
+        gat4.put(n, dh32[half_rows(n), :] + scale1 * (e1 - z1 * jnp.mean(e1 * z1, axis=-1, keepdims=True)))
+    rs_o.step3()
+    rs_g.step3()
+    rs_q.step3()
+    rs_kvw.step3()
+    for a in rs_m:
+        a.step4()
+
+    def keep(ref, base=0):
+        def store(rows, v):
+            ref[pl.ds(rows.start + base, rows.size), :] = v
+
+        return store
+
+    for n in (0, 1):
+        gat2.step(n)
+    for n in (0, 1):
+        rs_d[n].finish(keep(md_f, 384 * n))
     move(md_f, md_out)
-    rs_mg.finish(keep(mg_f))
-    move(mg_f, mg_out)
-    gat2.step()
+    rs_o.step4()
+    rs_g.step4()
+    rs_q.step4()
     rs_kvw.step4()
-    rs_q.step4()
     net.wait_came(gzr, sz[1])
     gy[y] = gx1[z] + gzr[0] + gzr[1] + gzr[2]
     for d in (1, 2, 3):
         net.send(gy.at[y], gy.at[y], net.at(dy=d), *sy)
-    rs_mu.finish(keep(mu_f))
+    for n in (0, 1):
+        gat4.step(n)
+    rs_m[0].finish(keep(mg_f))
+    move(mg_f, mg_out)
+    rs_m[1].finish(keep(mu_f))
     move(mu_f, mu_out)
-    rs_o.finish(keep(og_f))
-    move(og_f, og_out)
-    rs_g.finish(keep(gg_f))
-    move(gg_f, gg_out)
-    gat4.step()
-
-    def store_kvw(rows, v):
-        kg_f[rows, :] = v[:, :128]
-        vg_f[rows, :] = v[:, 128:]
-
     gat2.finish()
     move(bo, bo_out)
     net.wait_came(gy.at[0:3], sy[1])
     gc[c] = gy[0] + gy[1] + gy[2] + gy[3]
     net.send(gc.at[c], gc.at[c], net.at(dc=1), *sc)
+    rs_o.finish(keep(og_f))
+    move(og_f, og_out)
+    rs_g.finish(keep(gg_f))
+    move(gg_f, gg_out)
     rs_q.finish(keep(qg_f))
     move(qg_f, qg_out)
+    gat4.finish()
+    move(igb, ig_out)
+
+    def store_kvw(rows, v):
+        kg_f[rows, :] = v[:, :128]
+        vg_f[rows, :] = v[:, 128:]
+
     rs_kvw.finish(store_kvw)
     move(kg_f, kg_out)
     move(vg_f, vg_out)
-    gat4.finish()
-    move(igb, ig_out)
     net.wait_came(gc.at[0], sc[1])
     gn_f[...] = gc[0] + gc[1]
     move(gn_f.at[pl.ds(0, 1)], gain1_out)
     move(gn_f.at[pl.ds(1, 1)], gain2_out)
-    for a in (rs_mg, rs_mu, rs_d, rs_kv, rs_g, rs_q, rs_o, rs_kvw, red2, red4, gat, gat2, gat3, gat4):
+    for a in (*rs_m, *rs_d, *rs_kv, rs_g, rs_q, rs_o, rs_kvw, red2, red4, gat, gat2, gat3, gat4):
         a.drain()
     net.wait_sent(gxr, sx[0])
     net.wait_sent(gzr, sz[0])
@@ -786,6 +811,8 @@
         v((4, 4, 768, 128), BF16),
         v((4, 4, 256, 256), BF16),
         v((4, 4, 256, 256), BF16),
+        v((4, 4, 384, 128), BF16),
+        v((4, 4, 384, 128), BF16),
         v((256, 2048), BF16),
         v((256, 2048), BF16),
         v((2048, 256), BF16),
@@ -825,9 +852,9 @@
     ]
     grad_shapes = ((128, 768), (128, 768), (768, 128), (256, 128), (128, 256), (128, 256), (128, 128), (128, 128), (8, 128))
     scratch += [v(dims, F32) for dims in grad_shapes]
-    for rows, cols in ((768, 128), (128, 768), (128, 768), (256, 256), (256, 128), (128, 256), (128, 256), (128, 256)):
+    for rows, cols in ((384, 128), (384, 128), (128, 768), (128, 768), (256, 128), (256, 128), (128, 256), (128, 256), (128, 256), (256, 128)):
         scratch += scatter_bufs(rows, cols)
-    scratch += [pltpu.SemaphoreType.DMA((324,)), pltpu.SemaphoreType.DMA((24,))]
+    scratch += [pltpu.SemaphoreType.DMA((188,)), pltpu.SemaphoreType.DMA((24,))]
     whole = pl.BlockSpec(memory_space=pltpu.VMEM)
     there = pl.BlockSpec(memory_space=pl.ANY)
     shape = jax.ShapeDtypeStruct

time: 191 us -> 182 us (0.953)
  Pallas kernels: 190 us -> 181 us
    pallas_call x1, Pallas kernels: 186 us -> 177 us  [per_device(): pl.pallas_call(kernel, out_shape=(shape(y_rows, BF16), shape(y_rows, BF16...]
where the time goes in v3:
time: 182 us
  Pallas kernels  181 us (99%)
    pallas_call x1, Pallas kernels, per_device(): pl.pallas_call(kernel, out_shape=(shape(y_rows, BF16), shape(y_rows, BF16...  177 us

profile of v3, /device:TPU:1, one launch (start us, length us, event | category | flops | bytes accessed | tf_op | source)
XLA Modules:
  0.0 181.8 jit_solution(2632148201342293102)
XLA Ops:
  0.6 177.5 %shard_map.220 = (bf16[4,2,32,2048]{3,2,1,0:T(8,128)(2,1)}, bf16[4,2,32,2048]{3,2,1,0:T(8,128)(2,1)}, f32[1,128]{1,0:T(1,128)}, f32[128,256]{1,0:T(8,128)}, f32[...) custom-call(bf16[256,2048]{1,0:T(8,128)(2,1)} %refs_0_.1, ...), custom_call_target="tpu_custom_call" | custom-call | tf_op jit(solution)/shard_map/pallas_call | solution.py:875
  178.1 3.5 %shard_map.221 = (bf16[256,2048]{1,0:T(8,128)(2,1)}, f32[256,2048]{1,0:T(8,128)}, f32[1,128]{1,0:T(1,128)}, f32[128,256]{1,0:T(8,128)}, f32[128,256]{1,0:T(8,128...) custom-call(bf16[256,2048]{1,0:T(8,128)(2,1)} %bitcast.7, ...), custom_call_target="tpu_custom_call" | custom-call | tf_op jit(solution)/shard_map/pallas_call | solution.py:897

commit v4 on v3

--- a/solution.py
+++ b/solution.py
@@ -323,7 +323,8 @@
     r1c, gp, ob, ot, qt, dot_, dqt, dmb, ab, dadu, mt = take(11)
     h32, z32, r32, dh32 = take(4)
     gx0, gxr, gx1, gzr, gy, gc = take(6)
-    mg_f, mu_f, md_f, og_f, qg_f, gg_f, kg_f, vg_f, gn_f = take(9)
+    md_f, og_f, qg_f, gg_f, kg_f, vg_f, gn_f = take(7)
+    mg_f, mu_f = ab.at[0:128], ab.at[128:256]
     sb = [take(4) for _ in range(10)]
     sems, local = take(2)
 
@@ -774,27 +775,18 @@
 
 
 def place_outputs(*refs):
-    ins, outs, bufs, (wide, sems) = refs[:12], refs[12:24], refs[24:36], refs[36:]
+    ins, outs, (narrow, wide, sems) = refs[:12], refs[12:24], refs[24:]
     spans = [pl.ds(64 * i, 64) for i in range(4)]
-    loads = [pltpu.make_async_copy(ins[1].at[r], bufs[1].at[r], sems.at[i]) for i, r in enumerate(spans)]
-    order = [0, 9, 10, 11, 3, 4, 5, 6, 7, 2, 8]
-    rest = [pltpu.make_async_copy(ins[i], bufs[i], sems.at[4 + i]) for i in order]
-    for d in loads + rest:
+    loads = [pltpu.make_async_copy(ins[1].at[r], narrow.at[r], sems.at[i]) for i, r in enumerate(spans)]
+    copies = [pltpu.make_async_copy(ins[i], outs[i], sems.at[4 + i]) for i in (0, 9, 10, 11, 3, 4, 5, 6, 7, 2, 8)]
+    for d in loads + copies:
         d.start()
-    copies = []
-
-    def out(src, dst, n):
-        d = pltpu.make_async_copy(src, dst, sems.at[n])
+    for i, r in enumerate(spans):
+        loads[i].wait()
+        wide[r, :] = narrow[r, :].astype(F32)
+        d = pltpu.make_async_copy(wide.at[r], outs[1].at[r], sems.at[16 + i])
         d.start()
         copies.append(d)
-
-    for i, r in enumerate(spans):
-        loads[i].wait()
-        wide[r, :] = bufs[1][r, :].astype(F32)
-        out(wide.at[r], outs[1].at[r], 16 + i)
-    for i, d in zip(order, rest):
-        d.wait()
-        out(bufs[i], outs[i], 20 + i)
     for d in copies:
         d.wait()
 
@@ -850,7 +842,7 @@
         v((4, 8, 128), F32),
         v((2, 8, 128), F32),
     ]
-    grad_shapes = ((128, 768), (128, 768), (768, 128), (256, 128), (128, 256), (128, 256), (128, 128), (128, 128), (8, 128))
+    grad_shapes = ((768, 128), (256, 128), (128, 256), (128, 256), (128, 128), (128, 128), (8, 128))
     scratch += [v(dims, F32) for dims in grad_shapes]
     for rows, cols in ((384, 128), (384, 128), (128, 768), (128, 768), (256, 128), (256, 128), (128, 256), (128, 256), (128, 256), (256, 128)):
         scratch += scatter_bufs(rows, cols)
@@ -874,11 +866,11 @@
     )
     outs = pl.pallas_call(
         kernel,
-        out_shape=(shape(y_rows, BF16), shape(y_rows, BF16)) + out_shape[2:],
+        out_shape=tuple(v(o.shape, o.dtype) for o in (shape(y_rows, BF16), shape(y_rows, BF16)) + out_shape[2:]),
         in_specs=[there, there, whole, whole, whole] + [there] * 8,
         out_specs=[there] * 12,
         scratch_shapes=scratch,
-        compiler_params=pltpu.CompilerParams(collective_id=0, has_side_effects=True, vmem_limit_bytes=63 << 20),
+        compiler_params=pltpu.CompilerParams(collective_id=0, has_side_effects=True, vmem_limit_bytes=58 << 20),
     )(
         inputs,
         cotangent,
@@ -899,8 +891,8 @@
         out_shape=out_shape,
         in_specs=[there] * 12,
         out_specs=[there] * 12,
-        scratch_shapes=[v(o.shape, BF16 if i == 1 else o.dtype) for i, o in enumerate(out_shape)] + [v((256, 2048), F32), pltpu.SemaphoreType.DMA((32,))],
-        compiler_params=pltpu.CompilerParams(vmem_limit_bytes=60 << 20),
+        scratch_shapes=[v((256, 2048), BF16), v((256, 2048), F32), pltpu.SemaphoreType.DMA((20,))],
+        compiler_params=pltpu.CompilerParams(vmem_limit_bytes=8 << 20),
     )(outs[0].reshape(256, 2048), outs[1].reshape(256, 2048), *outs[2:])
     outs = list(outs)
     outs[2] = outs[2].reshape(128)

time: 182 us -> 180 us (0.989)
  Pallas kernels: 181 us -> 179 us
where the time goes in v4:
time: 180 us
  Pallas kernels  179 us (99%)
    pallas_call x1, Pallas kernels, per_device(): pl.pallas_call(kernel, out_shape=tuple((v(o.shape, o.dtype) for o in (sha...  177 us

profile of v4, /device:TPU:1, one launch (start us, length us, event | category | flops | bytes accessed | tf_op | source)
XLA Modules:
  0.0 180.3 jit_solution(15842982749139652271)
XLA Ops:
  0.6 177.0 %shard_map.220 = (bf16[4,2,32,2048]{3,2,1,0:T(8,128)(2,1)S(1)}, bf16[4,2,32,2048]{3,2,1,0:T(8,128)(2,1)S(1)}, f32[1,128]{1,0:T(1,128)S(1)}, f32[128,256]{1,0:T(8...) custom-call(bf16[256,2048]{1,0:T(8,128)(2,1)} %refs_0_.1, ...), custom_call_target="tpu_custom_call" | custom-call | tf_op jit(solution)/shard_map/pallas_call | solution.py:867
  177.6 2.5 %shard_map.221 = (bf16[256,2048]{1,0:T(8,128)(2,1)}, f32[256,2048]{1,0:T(8,128)}, f32[1,128]{1,0:T(1,128)}, f32[128,256]{1,0:T(8,128)}, f32[128,256]{1,0:T(8,128...) custom-call(bf16[256,2048]{1,0:T(8,128)(2,1)S(1)} %bitcast.7, ...), custom_call_target="tpu_custom_call" | custom-call | tf_op jit(solution)/shard_map/pallas_call | solution.py:889

commit v5 on v4

--- a/solution.py
+++ b/solution.py
@@ -775,16 +775,14 @@
 
 
 def place_outputs(*refs):
-    ins, outs, (narrow, wide, sems) = refs[:12], refs[12:24], refs[24:]
-    spans = [pl.ds(64 * i, 64) for i in range(4)]
-    loads = [pltpu.make_async_copy(ins[1].at[r], narrow.at[r], sems.at[i]) for i, r in enumerate(spans)]
-    copies = [pltpu.make_async_copy(ins[i], outs[i], sems.at[4 + i]) for i in (0, 9, 10, 11, 3, 4, 5, 6, 7, 2, 8)]
-    for d in loads + copies:
+    ins, outs, (wide, sems) = refs[:12], refs[12:24], refs[24:]
+    copies = [pltpu.make_async_copy(ins[i], outs[i], sems.at[i]) for i in (0, 9, 10, 11, 3, 4, 5, 6, 7, 2, 8)]
+    for d in copies:
         d.start()
-    for i, r in enumerate(spans):
-        loads[i].wait()
-        wide[r, :] = narrow[r, :].astype(F32)
-        d = pltpu.make_async_copy(wide.at[r], outs[1].at[r], sems.at[16 + i])
+    for i in range(4):
+        r = pl.ds(64 * i, 64)
+        wide[r, :] = ins[1][r, :].astype(F32)
+        d = pltpu.make_async_copy(wide.at[r], outs[1].at[r], sems.at[12 + i])
         d.start()
         copies.append(d)
     for d in copies:
@@ -889,9 +887,9 @@
     outs = pl.pallas_call(
         place_outputs,
         out_shape=out_shape,
-        in_specs=[there] * 12,
+        in_specs=[there, whole] + [there] * 10,
         out_specs=[there] * 12,
-        scratch_shapes=[v((256, 2048), BF16), v((256, 2048), F32), pltpu.SemaphoreType.DMA((20,))],
+        scratch_shapes=[v((256, 2048), F32), pltpu.SemaphoreType.DMA((16,))],
         compiler_params=pltpu.CompilerParams(vmem_limit_bytes=8 << 20),
     )(outs[0].reshape(256, 2048), outs[1].reshape(256, 2048), *outs[2:])
     outs = list(outs)

time: 180 us -> 180 us (level)
  no operation moved by 1% of the time
where the time goes in v5:
time: 180 us
  Pallas kernels  179 us (99%)
    pallas_call x1, Pallas kernels, per_device(): pl.pallas_call(kernel, out_shape=tuple((v(o.shape, o.dtype) for o in (sha...  177 us

profile of v5, /device:TPU:1, one launch (start us, length us, event | category | flops | bytes accessed | tf_op | source)
XLA Modules:
  0.0 180.2 jit_solution(10841460415479704698)
XLA Ops:
  0.6 177.0 %shard_map.220 = (bf16[4,2,32,2048]{3,2,1,0:T(8,128)(2,1)S(1)}, bf16[4,2,32,2048]{3,2,1,0:T(8,128)(2,1)S(1)}, f32[1,128]{1,0:T(1,128)S(1)}, f32[128,256]{1,0:T(8...) custom-call(bf16[256,2048]{1,0:T(8,128)(2,1)} %refs_0_.1, ...), custom_call_target="tpu_custom_call" | custom-call | tf_op jit(solution)/shard_map/pallas_call | solution.py:865
  177.6 2.4 %shard_map.221 = (bf16[256,2048]{1,0:T(8,128)(2,1)}, f32[256,2048]{1,0:T(8,128)}, f32[1,128]{1,0:T(1,128)}, f32[128,256]{1,0:T(8,128)}, f32[128,256]{1,0:T(8,128...) custom-call(bf16[256,2048]{1,0:T(8,128)(2,1)S(1)} %bitcast.7, ...), custom_call_target="tpu_custom_call" | custom-call | tf_op jit(solution)/shard_map/pallas_call | solution.py:887
